TPU v7x, 512 devices: a whole 4x8x8 slice. The times are simulated.
512 devices in a mesh: lat: 16 (over y_lo, x, core), lon: 32 (over z, y_hi).
Axes of the slice: x: 4, y: 8 (y_hi: 4, y_lo: 2; y = y_hi * 2 + y_lo), z: 8, core: 2. Of those that a mesh axis runs over, the one named last changes fastest.
Arguments:
- tokens: bfloat16 [2, 96, 73728], P(None, 'lat', 'lon'), may hold values from -6 to 6
- labels: int32 [2, 96, 384], P(None, 'lat', 'lon'), may hold values from 0 to 3, as said below
- norm1_gain: float32 [192], replicated, may hold values from 0.1 to 1.9
- qkv_weight: bfloat16 [192, 576], replicated, may hold values from -0.4375 to 0.4375
- proj_weight: bfloat16 [192, 192], replicated, may hold values from -0.4375 to 0.4375
- bias_table: float32 [16, 6, 23, 144], P('lat'), may hold values from -3 to 350
- norm2_gain: float32 [192], replicated, may hold values from 0.1 to 1.9
- up_weight: bfloat16 [192, 768], replicated, may hold values from -0.4375 to 0.4375
- down_weight: bfloat16 [768, 192], replicated, may hold values from -0.21875 to 0.21875
- cotangent: bfloat16 [2, 96, 73728], P(None, 'lat', 'lon'), may hold values from -6 to 6
Outputs:
- block_out: bfloat16 [2, 96, 73728], P(None, 'lat', 'lon')
- token_grad: bfloat16 [2, 96, 73728], P(None, 'lat', 'lon')
- norm1_grad: float32 [192], replicated
- qkv_grad: float32 [192, 576], replicated
- proj_grad: float32 [192, 192], replicated
- bias_grad: float32 [16, 6, 23, 144], P('lat')
- norm2_grad: float32 [192], replicated
- up_grad: float32 [192, 768], replicated
- down_grad: float32 [768, 192], replicated
Inputs may be any that keep to these rules, and one draw needn't show every extreme that they name: `labels`: A cell of the rolled frame in the last 3 latitude rows has an odd label and every other cell an even one.
All inputs are finite; a program needn't handle non-finite values.
Results may differ from a plain program's by a relative error of at most 0.023.
Values may be sent and summed in bfloat16 or wider, within the bound.
A program may use at most 64 MiB of HBM per device.

v0:
```python
import jax
import jax.numpy as jnp
from jax import lax
from jax.sharding import PartitionSpec as P

HEADS = 6


norm_eps = 1e-05
gelu_coeff = 0.044715
root_two_over_pi = 0.7978845608028654
masked_score = -1e30


def shifted(block, axis, distance):
    devices = range(lax.axis_size(axis))
    route = [((i - distance) % len(devices), i) for i in devices]
    return lax.ppermute(block, axis, route)


def layer_norm(values, gain_vec):
    center = values - jnp.mean(values, axis=-1, keepdims=True)
    inv_std = lax.rsqrt(jnp.mean(center * center, axis=-1, keepdims=True) + norm_eps)
    normal_part = center * inv_std
    return (normal_part * gain_vec, normal_part, inv_std)


def norm_back(grad_out, normal_part, inv_std, gain_vec):
    scaled = grad_out * gain_vec
    grad_in = inv_std * (
        scaled
        - jnp.mean(scaled, axis=-1, keepdims=True)
        - normal_part * jnp.mean(scaled * normal_part, axis=-1, keepdims=True)
    )
    return (grad_in, jnp.sum(grad_out * normal_part, axis=0))


def gelu_value(pre_act):
    tanh_part = jnp.tanh(root_two_over_pi * (pre_act + gelu_coeff * pre_act * pre_act * pre_act))
    return 0.5 * pre_act * (1.0 + tanh_part)


def gelu_slope(pre_act):
    tanh_part = jnp.tanh(root_two_over_pi * (pre_act + gelu_coeff * pre_act * pre_act * pre_act))
    return 0.5 * (1.0 + tanh_part) + 0.5 * pre_act * (
        1.0 - tanh_part * tanh_part
    ) * root_two_over_pi * (1.0 + 3.0 * gelu_coeff * pre_act * pre_act)


def lon_table():
    offsets = jnp.arange(144, dtype=jnp.int32)
    spread = offsets % 12 - offsets // 12 + 11
    return (spread[:, None] == jnp.arange(23, dtype=jnp.int32)[None, :]).astype(jnp.float32)


def expand_bias(table_band):
    full_bias = jnp.einsum("hdp,ed->hpe", table_band, lon_table(), precision=lax.Precision.HIGHEST)
    head_count = full_bias.shape[0]
    full_bias = full_bias.reshape(head_count, 2, 6, 2, 6, 12, 12).transpose(0, 1, 2, 5, 3, 4, 6)
    return full_bias.reshape(head_count, 144, 144)


def fold_bias(grad_full):
    head_count = grad_full.shape[0]
    folded = grad_full.reshape(head_count, 2, 6, 12, 2, 6, 12).transpose(0, 1, 2, 4, 5, 3, 6)
    folded = folded.reshape(head_count, 144, 144)
    return jnp.einsum("hpe,ed->hdp", folded, lon_table(), precision=lax.Precision.HIGHEST)


def to_windows(frame_data):
    level_count, lat_cells, lon_cells, features = frame_data.shape
    blocks = frame_data.reshape(level_count, lat_cells // 6, 6, lon_cells // 12, 12, features)
    return blocks.transpose(1, 3, 0, 2, 4, 5).reshape(
        lat_cells // 6, lon_cells // 12, level_count * 72, features
    )


def from_windows(windows, level_count):
    lat_wins, lon_wins, window_cells, features = windows.shape
    blocks = windows.reshape(lat_wins, lon_wins, level_count, 6, 12, features).transpose(
        2, 0, 3, 1, 4, 5
    )
    return blocks.reshape(level_count, lat_wins * 6, lon_wins * 12, features)


def attend(packed, table_band, labels_band):
    lon_wins, window_cells, triple = packed.shape
    features = triple // 3
    head_size = features // HEADS
    split_parts = packed.reshape(lon_wins, window_cells, 3, HEADS, head_size)
    scores = jnp.einsum(
        "bqhd,bkhd->bhqk",
        split_parts[:, :, 0],
        split_parts[:, :, 1],
        preferred_element_type=jnp.float32,
    )
    scores = scores * head_size ** (-0.5) + expand_bias(table_band)[None]
    same_label = labels_band[:, :, None] == labels_band[:, None, :]
    scores = jnp.where(same_label[:, None], scores, masked_score)
    weights = jnp.exp(scores - jnp.max(scores, axis=-1, keepdims=True))
    weights = weights / jnp.sum(weights, axis=-1, keepdims=True)
    mixed_heads = jnp.einsum(
        "bhqk,bkhd->bqhd",
        weights.astype(jnp.bfloat16),
        split_parts[:, :, 2],
        preferred_element_type=jnp.float32,
    )
    return (mixed_heads.astype(jnp.bfloat16).reshape(lon_wins, window_cells, features), weights)


def attend_back(packed, weights, grad_mixed):
    lon_wins, window_cells, triple = packed.shape
    features = triple // 3
    head_size = features // HEADS
    split_parts = packed.reshape(lon_wins, window_cells, 3, HEADS, head_size)
    queries, keys, values = (split_parts[:, :, 0], split_parts[:, :, 1], split_parts[:, :, 2])
    grad_heads = grad_mixed.reshape(lon_wins, window_cells, HEADS, head_size)
    grad_weights = jnp.einsum(
        "bqhd,bkhd->bhqk", grad_heads, values, preferred_element_type=jnp.float32
    )
    grad_values = jnp.einsum(
        "bhqk,bqhd->bkhd",
        weights.astype(jnp.bfloat16),
        grad_heads,
        preferred_element_type=jnp.float32,
    )
    grad_scores = weights * (grad_weights - jnp.sum(weights * grad_weights, axis=-1, keepdims=True))
    grad_scaled = (grad_scores * head_size ** (-0.5)).astype(jnp.bfloat16)
    grad_queries = jnp.einsum(
        "bhqk,bkhd->bqhd", grad_scaled, keys, preferred_element_type=jnp.float32
    )
    grad_keys = jnp.einsum(
        "bhqk,bqhd->bkhd", grad_scaled, queries, preferred_element_type=jnp.float32
    )
    grad_packed = jnp.stack([grad_queries, grad_keys, grad_values], axis=2)
    grad_packed = grad_packed.reshape(lon_wins, window_cells, triple).astype(jnp.bfloat16)
    return (grad_packed, fold_bias(jnp.sum(grad_scores, axis=0)))


def feed_forward(residual, grad_out, gain_vec, up_weight, down_weight):
    normed, normal_part, inv_std = layer_norm(residual, gain_vec)
    normed = normed.astype(jnp.bfloat16)
    pre_act = jnp.dot(normed, up_weight, preferred_element_type=jnp.float32)
    hidden = gelu_value(pre_act).astype(jnp.bfloat16)
    block_rows = (
        residual + jnp.dot(hidden, down_weight, preferred_element_type=jnp.float32)
    ).astype(jnp.bfloat16)
    grad_hidden = jnp.einsum("rc,fc->rf", grad_out, down_weight, preferred_element_type=jnp.float32)
    down_grad = jnp.einsum("rf,rc->fc", hidden, grad_out, preferred_element_type=jnp.float32)
    grad_pre = (grad_hidden * gelu_slope(pre_act)).astype(jnp.bfloat16)
    up_grad = jnp.einsum("rc,rf->cf", normed, grad_pre, preferred_element_type=jnp.float32)
    grad_normed = jnp.einsum("rf,cf->rc", grad_pre, up_weight, preferred_element_type=jnp.float32)
    grad_in, gain_grad = norm_back(grad_normed, normal_part, inv_std, gain_vec)
    return (block_rows, grad_out.astype(jnp.float32) + grad_in, gain_grad, up_grad, down_grad)


def enter_frame(frame_data, lat_dim, strip_width, move_lat, move_lon):
    lat_cells = frame_data.shape[lat_dim]
    last_dim = frame_data.ndim - 1
    border = lax.slice_in_dim(frame_data, 0, 3, axis=lat_dim)
    frame_data = jnp.concatenate(
        [lax.slice_in_dim(frame_data, 3, lat_cells, axis=lat_dim), move_lat(border)], axis=lat_dim
    )
    border = lax.slice_in_dim(frame_data, 0, strip_width, axis=last_dim)
    lon_extent = frame_data.shape[last_dim]
    return jnp.concatenate(
        [lax.slice_in_dim(frame_data, strip_width, lon_extent, axis=last_dim), move_lon(border)],
        axis=last_dim,
    )


def leave_frame(frame_data, lat_dim, strip_width, move_lat, move_lon):
    last_dim = frame_data.ndim - 1
    lon_extent = frame_data.shape[last_dim]
    border = lax.slice_in_dim(frame_data, lon_extent - strip_width, lon_extent, axis=last_dim)
    frame_data = jnp.concatenate(
        [
            move_lon(border),
            lax.slice_in_dim(frame_data, 0, lon_extent - strip_width, axis=last_dim),
        ],
        axis=last_dim,
    )
    lat_cells = frame_data.shape[lat_dim]
    border = lax.slice_in_dim(frame_data, lat_cells - 3, lat_cells, axis=lat_dim)
    return jnp.concatenate(
        [move_lat(border), lax.slice_in_dim(frame_data, 0, lat_cells - 3, axis=lat_dim)],
        axis=lat_dim,
    )


def pull_lat_rows(border_piece):
    return shifted(border_piece, "lat", -1)


def pull_lon_columns(border_piece):
    return shifted(border_piece, "lon", -1)


def push_lat_rows(border_piece):
    return shifted(border_piece, "lat", 1)


def push_lon_columns(border_piece):
    return shifted(border_piece, "lon", 1)


def on_device(
    tokens,
    labels,
    norm1_gain,
    qkv_weight,
    proj_weight,
    bias_table,
    norm2_gain,
    up_weight,
    down_weight,
    cotangent,
):
    level_count, lat_cells, flat_extent = tokens.shape
    features = norm1_gain.shape[0]
    lon_cells = flat_extent // features
    strip_width = 6 * features
    shifted_tokens = enter_frame(tokens, 1, strip_width, pull_lat_rows, pull_lon_columns)
    window_tokens = to_windows(shifted_tokens.reshape(level_count, lat_cells, lon_cells, features))
    lat_wins, lon_wins, window_cells = window_tokens.shape[:3]
    window_labels = to_windows(labels[..., None])[..., 0]
    token_rows = window_tokens.reshape(-1, features).astype(jnp.float32)
    normed, normal_one, inv_one = layer_norm(token_rows, norm1_gain)
    normed = normed.astype(jnp.bfloat16)
    packed = jnp.dot(normed, qkv_weight, preferred_element_type=jnp.float32).astype(jnp.bfloat16)
    packed = packed.reshape(lat_wins, lon_wins, window_cells, 3 * features)
    mixed_heads, weights = jax.vmap(attend)(packed, bias_table, window_labels)
    mixed_rows = mixed_heads.reshape(-1, features)
    branch = jnp.dot(mixed_rows, proj_weight, preferred_element_type=jnp.float32).astype(
        jnp.bfloat16
    )
    frame_branch = from_windows(
        branch.reshape(lat_wins, lon_wins, window_cells, features), level_count
    )
    frame_branch = leave_frame(
        frame_branch.reshape(level_count, lat_cells, flat_extent),
        1,
        strip_width,
        push_lat_rows,
        push_lon_columns,
    )
    residual = (tokens.astype(jnp.float32) + frame_branch.astype(jnp.float32)).reshape(-1, features)
    grad_rows = cotangent.reshape(-1, features)
    block_rows, grad_resid, gain_two, up_grad, down_grad = feed_forward(
        residual, grad_rows, norm2_gain, up_weight, down_weight
    )
    grad_branch = grad_resid.astype(jnp.bfloat16)
    moved_grad = enter_frame(
        grad_branch.reshape(level_count, lat_cells, flat_extent),
        1,
        strip_width,
        pull_lat_rows,
        pull_lon_columns,
    )
    branch_rows = to_windows(
        moved_grad.reshape(level_count, lat_cells, lon_cells, features)
    ).reshape(-1, features)
    proj_grad = jnp.einsum("rc,rd->cd", mixed_rows, branch_rows, preferred_element_type=jnp.float32)
    grad_mixed = jnp.einsum(
        "rc,dc->rd", branch_rows, proj_weight, preferred_element_type=jnp.float32
    ).astype(jnp.bfloat16)
    grad_packed, bias_grad = jax.vmap(attend_back)(
        packed, weights, grad_mixed.reshape(lat_wins, lon_wins, window_cells, features)
    )
    grad_packed = grad_packed.reshape(-1, 3 * features)
    qkv_grad = jnp.einsum("rc,rd->cd", normed, grad_packed, preferred_element_type=jnp.float32)
    grad_normed = jnp.einsum(
        "rc,dc->rd", grad_packed, qkv_weight, preferred_element_type=jnp.float32
    )
    grad_shift_in, gain_one = norm_back(grad_normed, normal_one, inv_one, norm1_gain)
    grad_shift_in = grad_shift_in.astype(jnp.bfloat16)
    frame_grad = from_windows(
        grad_shift_in.reshape(lat_wins, lon_wins, window_cells, features), level_count
    )
    frame_grad = leave_frame(
        frame_grad.reshape(level_count, lat_cells, flat_extent),
        1,
        strip_width,
        push_lat_rows,
        push_lon_columns,
    )
    token_grad = (
        grad_resid.reshape(level_count, lat_cells, flat_extent) + frame_grad.astype(jnp.float32)
    ).astype(jnp.bfloat16)
    block_out = block_rows.reshape(level_count, lat_cells, flat_extent)
    grad_scale = float(
        level_count * lat_cells * lon_cells * lax.axis_size("lat") * lax.axis_size("lon")
    ) ** (-0.5)
    totals = lax.psum((gain_one, qkv_grad, proj_grad, gain_two, up_grad, down_grad), ("lat", "lon"))
    bias_total = lax.psum(bias_grad.astype(jnp.bfloat16), "lon").astype(jnp.float32)
    return (
        block_out,
        token_grad,
        totals[0] * grad_scale,
        totals[1] * grad_scale,
        totals[2] * grad_scale,
        bias_total,
        totals[3] * grad_scale,
        totals[4] * grad_scale,
        totals[5] * grad_scale,
    )


def solution(mesh):
    in_specs = (
        P(None, "lat", "lon"),
        P(None, "lat", "lon"),
        P(),
        P(),
        P(),
        P("lat", None, None, None),
        P(),
        P(),
        P(),
        P(None, "lat", "lon"),
    )
    out_specs = (
        P(None, "lat", "lon"),
        P(None, "lat", "lon"),
        P(),
        P(),
        P(),
        P("lat", None, None, None),
        P(),
        P(),
        P(),
    )
    return jax.shard_map(
        on_device, mesh=mesh, in_specs=in_specs, out_specs=out_specs, check_vma=False
    )
```

profile of v0, /device:TPU:1, one launch (start us, length us, event | category | flops | bytes accessed | tf_op | source)
XLA Modules:
  0.0 510.1 jit_solution(1716366791517340043)
XLA Ops:
  8.1 8.8 %collective-permute-start = (bf16[2,3,2304]{2,0,1:T(2,128)(2,1)S(1)}, bf16[2,3,2304]{2,0,1:T(2,128)(2,1)S(1)}, u32[]{:S(2)}, u32[]{:S(2)}) collective-permute-start(bf16[2,3,2304]{2,0,1:T(2,128)(2,1)S(1)} %get-tuple-element.52), channel_id=1, source_target_pairs={{32,0},{64,32},{96,64},{128,96},{160,128},{192,160},{224,192},{256... | collective-permute-start | bytes 82952 | tf_op jit(solution)/shard_map/ppermute | solution.py:18
  19.0 9.5 %collective-permute-start.1 = (bf16[2,6,1152]{2,0,1:T(2,128)(2,1)S(1)}, bf16[2,6,1152]{2,0,1:T(2,128)(2,1)S(1)}, u32[]{:S(2)}, u32[]{:S(2)}) collective-permute-start(bf16[2,6,1152]{2,0,1:T(2,128)(2,1)S(1)} %get-tuple-element.50), channel_id=1, source_target_pairs={{1,0},{2,1},{3,2},{4,3},{5,4},{6,5},{7,6},{8,7},{9,8},{10,9},{11,1... | collective-permute-start | bytes 82952 | tf_op jit(solution)/shard_map/ppermute | solution.py:18
  28.5 5.0 convolution_bitcast_fusion
  33.6 11.3 %copy.67 = f32[1,6,2,6,12,2,6,12]{4,3,2,7,6,5,1,0:T(8,128)} copy(f32[1,6,2,6,12,2,6,12]{7,6,5,3,2,1,4,0:T(8,128)} %convolution_bitcast_fusion) | data formatting | bytes 995328 | tf_op jit(solution)/shard_map/vmap()/broadcast_in_dim;vmap()/reshape | solution.py:97
  44.9 5.0 reshape.384
  53.0 1.9 collective-permute-start.2
  57.9 4.0 collective-permute-done.2
  61.9 4.1 collective-permute-start.3
  75.2 6.7 %collective-permute-start.4 = (bf16[2,3,2304]{2,1,0:T(4,128)(2,1)S(1)}, bf16[2,3,2304]{2,1,0:T(4,128)(2,1)S(1)}, u32[]{:S(2)}, u32[]{:S(2)}) collective-permute-start(bf16[2,3,2304]{2,1,0:T(4,128)(2,1)S(1)} %get-tuple-element.46), channel_id=1, source_target_pairs={{32,0},{64,32},{96,64},{128,96},{160,128},{192,160},{224,192},{256... | collective-permute-start | bytes 82952 | tf_op jit(solution)/shard_map/ppermute | solution.py:18
  81.9 1.9 fusion.44
  83.8 2.6 collective-permute-start.5
  90.9 1.7 convolution_bitcast_fusion.1
  94.9 1.7 fusion.54
  99.7 3.5 collective-permute-start.6
  103.2 97.7 %all-reduce = (f32[192]{0:T(256)S(1)}, f32[192]{0:T(256)S(1)}) all-reduce(f32[192]{0:T(256)S(1)} %get-tuple-element.29, f32[192]{0:T(256)S(1)} %copy-done.9), channel_id=1, replica_groups=mesh['lat'=16,'lon'=32] {'lat','lon'}, use_global_device_ids=true, to_apply=%region_12.13 | all-reduce | flops 384 | bytes 3072 | tf_op jit(solution)/shard_map/psum | solution.py:294
  202.6 5.0 reshape.377
  207.6 8.4 %copy.58 = f32[1,6,2,6,2,6,12,12]{7,6,5,4,3,2,1,0:T(8,128)} copy(f32[1,6,2,6,2,6,12,12]{7,5,4,6,3,2,1,0:T(8,128)} %bitcast.97) | data formatting | bytes 995328 | tf_op jit(solution)/shard_map/vmap()/transpose | solution.py:65
  216.0 5.0 reshape.378
  222.1 3.0 collective-permute-start.7
  225.1 125.7 %psum.52 = bf16[1,6,23,144]{3,2,1,0:T(8,128)(2,1)S(1)} all-reduce(bf16[1,6,23,144]{3,2,1,0:T(8,128)(2,1)S(1)} %fusion.7), channel_id=1, replica_groups=mesh['lat'=16,'lon'=32] {'lon'}, use_global_device_ids=true, to_apply=%region_15.16 | all-reduce | flops 19872 | bytes 79488 | tf_op jit(solution)/shard_map/psum | solution.py:295
  352.3 143.6 %all-reduce.4.cloned.1.call-done = (f32[192,576]{1,0:T(8,128)}, f32[192,192]{1,0:T(8,128)}, f32[192,768]{1,0:T(8,128)}, f32[768,192]{0,1:T(8,128)}) async-done(((f32[192,576]{1,0:T(8,128)}, f32[192,192]{1,0:T(8,128)}, f32[192,768]{1,0:T(8,128)}, f32[768,192]{0,1:T(8,128)}), (f32[192,576]{1,0:T(8,128)}, f32[192,192]{1,0:T(8,128)}, f32[192,768]{1,0:T(8,128)}, ...) | async-done | bytes 1769488 | tf_op jit(solution)/shard_map/psum | solution.py:294
  495.9 1.9 broadcast_multiply_fusion.2
  499.4 1.9 broadcast_multiply_fusion.1
  501.4 1.9 broadcast_multiply_fusion
  (115 shorter events, 33.8 us)
Async XLA Ops:
  7.2 62.0 %copy-start = (bf16[192,768]{1,0:T(8,128)(2,1)S(1)}, bf16[192,768]{1,0:T(8,128)(2,1)}, u32[]{:S(2)}) copy-start(bf16[192,768]{1,0:T(8,128)(2,1)} %param.17) | copy-start | bytes 884740
  7.2 488.8 %all-reduce.4.cloned.1.call-start = ((), (), s32[]{:S(2)}) async-start(), calls=%async_computation | async-start | bytes 3735552 | tf_op jit(solution)/shard_map/psum | solution.py:294
  8.1 10.9 %collective-permute-start = (bf16[2,3,2304]{2,0,1:T(2,128)(2,1)S(1)}, bf16[2,3,2304]{2,0,1:T(2,128)(2,1)S(1)}, u32[]{:S(2)}, u32[]{:S(2)}) collective-permute-start(bf16[2,3,2304]{2,0,1:T(2,128)(2,1)S(1)} %get-tuple-element.52), channel_id=1, source_target_pairs={{32,0},{64,32},{96,64},{128,96},{160,128},{192,160},{224,192},{256... | collective-permute-start | bytes 82952 | tf_op jit(solution)/shard_map/ppermute | solution.py:18
  19.0 30.8 %collective-permute-start.1 = (bf16[2,6,1152]{2,0,1:T(2,128)(2,1)S(1)}, bf16[2,6,1152]{2,0,1:T(2,128)(2,1)S(1)}, u32[]{:S(2)}, u32[]{:S(2)}) collective-permute-start(bf16[2,6,1152]{2,0,1:T(2,128)(2,1)S(1)} %get-tuple-element.50), channel_id=1, source_target_pairs={{1,0},{2,1},{3,2},{4,3},{5,4},{6,5},{7,6},{8,7},{9,8},{10,9},{11,1... | collective-permute-start | bytes 82952 | tf_op jit(solution)/shard_map/ppermute | solution.py:18
  44.9 5.5 %copy-start.1 = (bf16[192,576]{1,0:T(8,128)(2,1)S(1)}, bf16[192,576]{1,0:T(8,128)(2,1)}, u32[]{:S(2)}) copy-start(bf16[192,576]{1,0:T(8,128)(2,1)} %param.13) | copy-start | bytes 663556
  44.9 5.6 %copy-start.7 = (f32[192]{0:T(256)S(1)}, f32[192]{0:T(256)}, u32[]{:S(2)}) copy-start(f32[192]{0:T(256)} %param.12) | copy-start | bytes 2308
  44.9 7.7 %copy-start.4 = (bf16[192,192]{1,0:T(8,128)(2,1)S(1)}, bf16[192,192]{1,0:T(8,128)(2,1)}, u32[]{:S(2)}) copy-start(bf16[192,192]{1,0:T(8,128)(2,1)} %param.14) | copy-start | bytes 221188
  52.0 0.6 copy-start.6
  52.4 5.0 copy-start.5
  53.0 8.9 %collective-permute-start.2 = (bf16[2,6,1152]{2,1,0:T(8,128)(2,1)S(1)}, bf16[2,6,1152]{2,1,0:T(8,128)(2,1)S(1)}, u32[]{:S(2)}, u32[]{:S(2)}) collective-permute-start(bf16[2,6,1152]{2,1,0:T(8,128)(2,1)S(1)} %get-tuple-element.47), channel_id=1, source_target_pairs={{31,0},{0,1},{1,2},{2,3},{3,4},{4,5},{5,6},{6,7},{7,8},{8,9},{9,10... | collective-permute-start | bytes 82952 | tf_op jit(solution)/shard_map/ppermute | solution.py:18
  61.9 5.9 %collective-permute-start.3 = (bf16[2,3,2304]{2,1,0:T(4,128)(2,1)S(1)}, bf16[2,3,2304]{2,1,0:T(4,128)(2,1)S(1)}, u32[]{:S(2)}, u32[]{:S(2)}) collective-permute-start(bf16[2,3,2304]{2,1,0:T(4,128)(2,1)S(1)} %fusion.26), channel_id=1, source_target_pairs={{480,0},{0,32},{32,64},{64,96},{96,128},{128,160},{160,192},{192,2... | collective-permute-start | bytes 82952 | tf_op jit(solution)/shard_map/ppermute | solution.py:18
  70.1 1.1 copy-start.3
  75.2 8.5 %collective-permute-start.4 = (bf16[2,3,2304]{2,1,0:T(4,128)(2,1)S(1)}, bf16[2,3,2304]{2,1,0:T(4,128)(2,1)S(1)}, u32[]{:S(2)}, u32[]{:S(2)}) collective-permute-start(bf16[2,3,2304]{2,1,0:T(4,128)(2,1)S(1)} %get-tuple-element.46), channel_id=1, source_target_pairs={{32,0},{64,32},{96,64},{128,96},{160,128},{192,160},{224,192},{256... | collective-permute-start | bytes 82952 | tf_op jit(solution)/shard_map/ppermute | solution.py:18
  83.8 5.7 %collective-permute-start.5 = (bf16[2,6,1152]{2,1,0:T(8,128)(2,1)S(1)}, bf16[2,6,1152]{2,1,0:T(8,128)(2,1)S(1)}, u32[]{:S(2)}, u32[]{:S(2)}) collective-permute-start(bf16[2,6,1152]{2,1,0:T(8,128)(2,1)S(1)} %get-tuple-element.44), channel_id=1, source_target_pairs={{1,0},{2,1},{3,2},{4,3},{5,4},{6,5},{7,6},{8,7},{9,8},{10,9},{11,1... | collective-permute-start | bytes 82952 | tf_op jit(solution)/shard_map/ppermute | solution.py:18
  90.9 7.2 %copy-start.8 = (f32[192]{0:T(256)S(1)}, f32[192]{0:T(256)}, u32[]{:S(2)}) copy-start(f32[192]{0:T(256)} %param.12) | copy-start | bytes 2308
  92.6 10.6 %copy-start.9 = (f32[192]{0:T(256)S(1)}, f32[192]{0:T(256)}, u32[]{:S(2)}) copy-start(f32[192]{0:T(256)} %get-tuple-element.27) | copy-start | bytes 2308
  99.7 122.3 %collective-permute-start.6 = (bf16[2,6,1152]{2,1,0:T(8,128)(2,1)S(1)}, bf16[2,6,1152]{2,1,0:T(8,128)(2,1)S(1)}, u32[]{:S(2)}, u32[]{:S(2)}) collective-permute-start(bf16[2,6,1152]{2,1,0:T(8,128)(2,1)S(1)} %get-tuple-element.41), channel_id=1, source_target_pairs={{31,0},{0,1},{1,2},{2,3},{3,4},{4,5},{5,6},{6,7},{7,8},{8,9},{9,10... | collective-permute-start | bytes 82952 | tf_op jit(solution)/shard_map/ppermute | solution.py:18
  216.0 5.6 %copy-start.10 = (s32[144]{0:T(256)S(1)}, s32[144]{0:T(256)}, u32[]{:S(2)}) copy-start(s32[144]{0:T(256)} %fusion.41) | copy-start | bytes 1732
  216.0 135.7 %copy-start.2 = (f32[2,6,2304]{2,1,0:T(8,128)S(1)}, f32[2,6,2304]{2,1,0:T(8,128)}, u32[]{:S(2)}) copy-start(f32[2,6,2304]{2,1,0:T(8,128)} %reshape.374) | copy-start | bytes 331780
  222.1 129.5 %collective-permute-start.7 = (bf16[2,3,2304]{2,1,0:T(4,128)(2,1)S(1)}, bf16[2,3,2304]{2,1,0:T(4,128)(2,1)S(1)}, u32[]{:S(2)}, u32[]{:S(2)}) collective-permute-start(bf16[2,3,2304]{2,1,0:T(4,128)(2,1)S(1)} %fusion.24), channel_id=1, source_target_pairs={{480,0},{0,32},{32,64},{64,96},{96,128},{128,160},{160,192},{192,2... | collective-permute-start | bytes 82952 | tf_op jit(solution)/shard_map/ppermute | solution.py:18
Sparse Core Ops, SparseCore 0:
  222.2 273.6 all-reduce.3
where the time goes:
time: 512 us; the launch traced here: 510 us
  blocking collectives  223 us (44%)
  waiting for transfers between devices  149 us (29%)
  local copies, waits for them, and re-layouts  44.7 us (9%)
  starting transfers between devices  40 us (8%)
  matrix products  23.4 us (5%)
  other arithmetic  14.6 us (3%)
  between operations  14.6 us (3%)
    psum x1, waiting for transfers between devices, on_device(): lax.psum((gain_one, qkv_grad, proj_grad, gain_two, up_grad, down_grad), (...  144 us
    psum x1, blocking collectives, on_device(): lax.psum(bias_grad.astype(jnp.bfloat16), 'lon').astype(jnp.float32)  126 us
    psum x1, blocking collectives, on_device(): lax.psum((gain_one, qkv_grad, proj_grad, gain_two, up_grad, down_grad), (...  97.7 us
    ppermute x8, starting transfers between devices, shifted(): return lax.ppermute(block, axis, route)  40 us
    reshape x2, local copies, waits for them, and re-layouts, attend(): scores = scores * head_size ** (-0.5) + expand_bias(table_band)[None]  16.3 us
  transfers between devices with their start and end apart: 9, of which 4 were waited for; matrix products, arithmetic and copies ran while one was open for 11% of the time, Pallas kernels for 0%

commit v1 on v0

v1 whole, which is shorter than its diff:
```python
import functools

import jax
import jax.numpy as jnp
from jax import lax
from jax.experimental import pallas as pl
from jax.experimental.pallas import tpu as pltpu
from jax.sharding import PartitionSpec as P

MESH = pl.DeviceIdType.MESH
F32, BF16 = jnp.float32, jnp.bfloat16
C, HEADS, FFN = 192, 6, 768
HALF = 6 * C
EPS = 1e-05
COEFF = 0.044715
ROOT = 0.7978845608028654
MASKED = -1e30
SCALE = 32.0**-0.5
ROWS_A, ROWS_C = 2304, 1792


def nn(a, b):
    return jnp.dot(a, b, preferred_element_type=F32)


def nt(a, b):
    return lax.dot_general(a, b, (((1,), (1,)), ((), ())), preferred_element_type=F32)


def tn(a, b):
    return lax.dot_general(a, b, (((0,), (0,)), ((), ())), preferred_element_type=F32)


def mean(x):
    return jnp.sum(x, axis=-1, keepdims=True) * (1.0 / C)


def norm(x, gain):
    center = x - mean(x)
    inv = lax.rsqrt(mean(center * center) + EPS)
    xhat = center * inv
    return (xhat * gain).astype(BF16), xhat, inv


def norm_back(grad, xhat, inv, gain):
    g = grad * gain
    grad_in = inv * (g - mean(g) - xhat * mean(g * xhat))
    return grad_in, jnp.sum(grad * xhat, axis=0, keepdims=True)


def iota(shape, dim):
    return lax.broadcasted_iota(jnp.int32, shape, dim)


def cell_row(rho):
    half, r = rho >> 3, rho & 7
    level = (r * 11) >> 5
    return level * 6 + half * 3 + r - level * 3, r < 6


def flat_pieces(per, start, rows):
    at = start
    while at < start + rows:
        take = min(per - at % per, start + rows - at)
        yield at - start, at // per, at % per, take
        at += take


def kernel(
    geo, tok, lab, g1, wqkv, wproj, btab, g2, wup, wdown, cot,
    o_block, o_token, o_n1, o_qkv, o_proj, o_bias, o_n2, o_up, o_down,
    stage, ent_s, ent_r, xs, gs, labs, ytab, bias, probs, ex_s, ex_r, rows_st,
    buf_a, buf_c, r1a, r1c, m1a, m1c, r2a, r2c, acc2, r3, z4, fin, nst,
    zfold, ffold, bst, b_s, b_r1, b_y, b_fin,
    *sems,
):
    nlat, nlon, ny_lo, nx, nz, ny_hi = geo
    ny = ny_lo * ny_hi
    pieces = 2 * nx
    ra, rc = ROWS_A // pieces, ROWS_C // pieces
    ry = (ra + rc) // ny
    cells = 144 * nlat * nlon
    (s_ent, s_exb, s_ext, s_1a, s_1c, s_2a, s_2c, s_3, s_4, s_5, s_6, s_7, s_b1, s_b2, s_b3) = [
        (sems[2 * i], sems[2 * i + 1]) for i in range(15)
    ]

    lat, lon = lax.axis_index("lat"), lax.axis_index("lon")
    core = lax.rem(lat, 2)
    x = lax.rem(lat // 2, nx)
    y_lo = lat // (2 * nx)
    z = lon // ny_hi
    y_hi = lax.rem(lon, ny_hi)
    y = y_hi * ny_lo + y_lo

    def at_core():
        return (lat + 1 - 2 * core, lon)

    def at_x(k):
        return ((y_lo * nx + lax.rem(x + k, nx)) * 2 + core, lon)

    def at_y(k):
        other = lax.rem(y + k, ny)
        return ((lax.rem(other, ny_lo) * nx + x) * 2 + core, z * ny_hi + other // ny_lo)

    def at_yhi(k):
        return (lat, z * ny_hi + lax.rem(y_hi + k, ny_hi))

    def at_z(k):
        return (lat, lax.rem(z + k, nz) * ny_hi + y_hi)

    def near(da, db):
        return (lax.rem(lat + da + nlat, nlat), lax.rem(lon + db + nlon, nlon))

    def push(src, dst, sem, i, dev):
        copy = pltpu.make_async_remote_copy(
            src_ref=src, dst_ref=dst, send_sem=sem[0].at[i], recv_sem=sem[1].at[i],
            device_id=dev, device_id_type=MESH,
        )
        copy.start()
        return copy

    barrier = pltpu.get_barrier_semaphore()
    partners = [at_core()]
    partners += [at_x(k) for k in range(1, nx)]
    partners += [at_y(k) for k in range(1, ny)]
    partners += [at_z(k) for k in range(1, nz)]
    partners += [near(-1, 0), near(0, -1), near(-1, -1), near(1, 0), near(0, 1), near(1, 1)]
    for dev in partners:
        pl.semaphore_signal(barrier, inc=1, device_id=dev, device_id_type=MESH)

    stage[...] = jnp.zeros_like(stage)
    for half in range(2):
        for part in range(2):
            for kind, ref in enumerate((tok, cot)):
                for level in range(2):
                    rows = ref[level].astype(F32)
                    stage[half * 2 + part, pl.ds(kind * 8 + level * 3, 3), :] = rows[
                        half * 3 : half * 3 + 3, part * HALF : (part + 1) * HALF
                    ]
    for i in range(3):
        ent_s[i] = stage[i].astype(BF16)
    pl.semaphore_wait(barrier, len(partners))
    entry = [
        push(ent_s.at[i], ent_r.at[i], s_ent, i, near(half - 1, part - 1))
        for i, (half, part) in enumerate(((0, 0), (0, 1), (1, 0)))
    ]

    labs[...] = jnp.full_like(labs, -1.0)
    for half in range(2):
        for level in range(2):
            labs[pl.ds(half * 8 + level * 3, 3), pl.ds(0, 12)] = lab[
                level, half * 3 : half * 3 + 3, :
            ].astype(F32)
    lab16 = labs[...].astype(BF16)
    pick = (11 - (iota((192, 128), 0) >> 4) == iota((192, 128), 1)).astype(F32).astype(BF16)
    lane_all = nt(lab16, pick)
    lane_lab = jnp.sum(
        jnp.where(iota((16, 192), 0) == (iota((16, 192), 1) & 15), lane_all, 0.0),
        axis=0, keepdims=True,
    )
    row_all = nt(pick, lab16)
    row_lab = jnp.sum(
        jnp.where(iota((192, 16), 1) == (iota((192, 16), 0) & 15), row_all, 0.0),
        axis=1, keepdims=True,
    )
    same = row_lab == lane_lab

    place, real = cell_row(iota((16, 144), 0))
    spot = iota((16, 144), 1)
    spot_row = (spot * 171) >> 11
    m1 = jnp.where((spot_row == place) & real, 1.0, 0.0)
    place_j, real_j = cell_row(iota((144, 192), 1) & 15)
    spot_j = iota((144, 192), 0)
    spot_col = spot_j - ((spot_j * 171) >> 11) * 12
    m2 = jnp.where((spot_col == place_j) & real_j, 1.0, 0.0).astype(BF16)
    group = iota((192, 192), 1) >> 4

    def build(h, carry):
        table = btab[0, h]
        left = table
        full = jnp.zeros((368, 192), F32)
        for _ in range(3):
            piece = left.astype(BF16).astype(F32)
            left = left - piece
            wide = (piece[:, None, :] * m1[None]).reshape(368, 144)
            full = full + nn(wide.astype(BF16), m2)
        ytab[...] = full
        out = ytab[pl.ds(176, 192), :]
        for bj in range(1, 12):
            out = jnp.where(group == bj, ytab[pl.ds((11 - bj) * 16, 192), :], out)
        bias[h] = jnp.where(same, out, MASKED)
        return carry

    lax.fori_loop(0, HEADS, build, 0)
    buf_c[...] = jnp.zeros_like(buf_c)
    nst[...] = jnp.zeros_like(nst)
    bst[...] = jnp.zeros_like(bst)

    def lay(quarter, half, part):
        for c in range(6):
            row = (11 - part * 6 - c) * 16 + half * 8
            xs[pl.ds(row, 8), :] = quarter[0:8, c * C : (c + 1) * C]
            gs[pl.ds(row, 8), :] = quarter[8:16, c * C : (c + 1) * C]

    lay(stage[3], 0, 0)
    for i, (half, part) in enumerate(((1, 1), (1, 0), (0, 1))):
        entry[i].wait()
        lay(ent_r[i].astype(F32), half, part)

    gain1, gain2 = g1[...], g2[...]
    tokens = xs[...]
    n1, xhat1, inv1 = norm(tokens, gain1)
    packed = nn(n1, wqkv[...]).astype(BF16)
    q, k, v = packed[:, :C], packed[:, C : 2 * C], packed[:, 2 * C :]
    head_of = iota((1, C), 1) >> 5
    masks = [(head_of == h).astype(F32).astype(BF16) for h in range(HEADS)]
    mixed = jnp.zeros((192, C), F32)
    for h in range(HEADS):
        s = nt(q * masks[h], k) * SCALE + bias[h]
        e = jnp.exp(s - jnp.max(s, axis=-1, keepdims=True))
        p = e * (1.0 / jnp.sum(e, axis=-1, keepdims=True))
        probs[h] = p
        mixed = mixed + nn(p.astype(BF16), v * masks[h])
    mixed = mixed.astype(BF16)
    branch = nn(mixed, wproj[...]).astype(BF16)
    residual = tokens + branch.astype(F32)
    n2, xhat2, inv2 = norm(residual, gain2)
    pre = nn(n2, wup[...])
    square = pre * pre
    tanh = jnp.tanh(ROOT * (pre + COEFF * pre * square))
    hidden = (0.5 * pre * (1.0 + tanh)).astype(BF16)
    slope = 0.5 * (1.0 + tanh) + 0.5 * pre * (1.0 - tanh * tanh) * ROOT * (
        1.0 + 3.0 * COEFF * square
    )
    block = residual + nn(hidden, wdown[...])

    def leave(which, value, sem):
        rows_st[...] = value
        copies = []
        for half in range(2):
            for part in range(2):
                i = half * 2 + part
                out = ex_r.at[which, 0] if i == 0 else ex_s.at[which, i]
                for c in range(6):
                    row = (11 - part * 6 - c) * 16 + half * 8
                    out[:, pl.ds(c * C, C)] = rows_st[pl.ds(row, 8), :]
                if i:
                    copies.append(
                        push(ex_s.at[which, i], ex_r.at[which, i], sem, i - 1, near(half, part))
                    )
        return copies

    exit_block = leave(0, block, s_exb)

    grads = gs[...]
    grads16 = grads.astype(BF16)
    grad_pre = (nt(grads16, wdown[...]) * slope).astype(BF16)
    down = tn(hidden, grads16)
    up = tn(n2, grad_pre)

    def put(buf, per, start, value, lanes=(0, 128)):
        value = value.astype(BF16)
        for src, piece, row, take in flat_pieces(per, start, value.shape[0]):
            buf[piece, pl.ds(row, take), pl.ds(lanes[0], lanes[1] - lanes[0])] = value[
                src : src + take
            ]

    for i in range(6):
        put(buf_a, ra, i * 192, up[:, i * 128 : (i + 1) * 128])
    put(buf_a, ra, 1152, down[:, :128])
    put(buf_a, ra, 1920, down[:384, 128:], (0, 64))
    put(buf_a, ra, 1920, down[384:, 128:], (64, 128))
    other = pl.ds((1 - core) * nx, nx)
    copy_1a = push(buf_a.at[other], r1a, s_1a, 0, at_core())

    grad_n2 = nt(grad_pre, wup[...])
    grad_in, norm2 = norm_back(grad_n2, xhat2, inv2, gain2)
    grad_res = grads + grad_in
    grad_branch = grad_res.astype(BF16)
    proj = tn(mixed, grad_branch)
    grad_mixed = nt(grad_branch, wproj[...]).astype(BF16)

    dq = jnp.zeros((192, C), F32)
    dk = jnp.zeros((192, C), F32)
    dv = jnp.zeros((192, C), F32)
    copies_2a = []
    for h in range(HEADS):
        gm = grad_mixed * masks[h]
        p = probs[h]
        dp = nt(gm, v)
        t = p * dp
        ds = ((t - p * jnp.sum(t, axis=-1, keepdims=True)) * SCALE).astype(BF16)
        zfold[h] = ds
        dv = dv + tn(p.astype(BF16), gm)
        dk = dk + tn(ds, q * masks[h])
        dq = dq + nn(ds, k * masks[h])
        if h == 1:
            copy_1a.wait()
            for i in range(nx):
                m1a[i] = (buf_a[core * nx + i].astype(F32) + r1a[i].astype(F32)).astype(BF16)
            copies_2a = [
                push(m1a.at[lax.rem(x + j, nx)], r2a.at[j - 1], s_2a, j - 1, at_x(j))
                for j in range(1, nx)
            ]
    grad_packed = jnp.concatenate([dq, dk, dv], axis=1).astype(BF16)
    qkv = tn(n1, grad_packed)
    grad_n1 = nt(grad_packed, wqkv[...])
    grad_in1, norm1 = norm_back(grad_n1, xhat1, inv1, gain1)

    for i in range(4):
        put(buf_c, rc, i * 192, qkv[:, i * 128 : (i + 1) * 128])
    put(buf_c, rc, 768, proj[:, :128])
    put(buf_c, rc, 960, qkv[:, 512:], (0, 64))
    put(buf_c, rc, 960, proj[:, 128:], (64, 128))
    nst[0:1, :] = norm1[:, :128]
    nst[1:2, 0:64] = norm1[:, 128:]
    nst[2:3, :] = norm2[:, :128]
    nst[3:4, 0:64] = norm2[:, 128:]
    put(buf_c, rc, 1152, nst[...])
    copy_1c = push(buf_c.at[other], r1c, s_1c, 0, at_core())

    token_grad = grad_res + grad_in1.astype(BF16).astype(F32)
    exit_token = leave(1, token_grad, s_ext)

    copy_1c.wait()
    for i in range(nx):
        m1c[i] = (buf_c[core * nx + i].astype(F32) + r1c[i].astype(F32)).astype(BF16)
    copies_2c = [
        push(m1c.at[lax.rem(x + j, nx)], r2c.at[j - 1], s_2c, j - 1, at_x(j)) for j in range(1, nx)
    ]

    def fold(h, carry):
        ds = zfold[h]
        ffold[...] = jnp.zeros_like(ffold)
        for bj in range(12):
            one = (iota((1, 192), 1) >> 4 == bj).astype(F32).astype(BF16)
            ffold[pl.ds((11 - bj) * 16, 192), :] += ds * one
        wide = nt(ffold[...], m2).reshape(23, 16, 144) * m1[None]
        o_bias[0, h] = jnp.sum(wide, axis=1) * (1.0 / SCALE)
        return carry

    lax.fori_loop(0, HEADS, fold, 0)
    for h in range(HEADS):
        bst[pl.ds(h * 24, 23), :] = o_bias[0, h, :, 0:128]
        bst[pl.ds(144, 23), pl.ds(h * 16, 16)] = o_bias[0, h, :, 128:144]
    rb = 256 // nz
    b_s[...] = bst[...].astype(BF16).reshape(nz, rb, 128)
    copies_b1 = [
        push(b_s.at[lax.rem(z + j, nz)], b_r1.at[j - 1], s_b1, j - 1, at_z(j)) for j in range(1, nz)
    ]

    def gather_sum(own, copies, slots):
        total = own.astype(F32)
        for i, copy in enumerate(copies):
            copy.wait()
            total = total + slots[i].astype(F32)
        return total.astype(BF16)

    own_a = m1a[x]
    acc2[pl.ds(0, ra), :] = gather_sum(own_a, copies_2a, r2a)
    acc2[pl.ds(ra, rc), :] = gather_sum(m1c[x], copies_2c, r2c)

    def part_y(ref, index):
        return ref.at[pl.ds(pl.multiple_of(index * ry, 16), ry)]

    copies_3 = [
        push(part_y(acc2, lax.rem(y + j, ny)), r3.at[j - 1], s_3, j - 1, at_y(j))
        for j in range(1, ny)
    ]

    b_y[y_hi] = gather_sum(b_s[z], copies_b1, b_r1)
    copies_b2 = [
        push(b_y.at[y_hi], b_y.at[y_hi], s_b2, j - 1, at_yhi(j)) for j in range(1, ny_hi)
    ]

    z4[z] = gather_sum(part_y(acc2, y)[...], copies_3, r3)
    copies_4 = [push(z4.at[z], z4.at[z], s_4, j - 1, at_z(j)) for j in range(1, nz)]

    for copy in copies_b2:
        copy.wait()
    total = b_y[0].astype(F32)
    for i in range(1, ny_hi):
        total = total + b_y[i].astype(F32)
    b_fin[z] = total.astype(BF16)
    copies_b3 = [push(b_fin.at[z], b_fin.at[z], s_b3, j - 1, at_z(j)) for j in range(1, nz)]

    for copy in copies_4:
        copy.wait()
    total = z4[0].astype(F32)
    for i in range(1, nz):
        total = total + z4[i].astype(F32)
    mine = core * nx + x
    done = part_y(fin.at[mine], y)
    done[...] = total.astype(BF16)
    copies_5 = [push(done, done, s_5, j - 1, at_y(j)) for j in range(1, ny)]

    def arrive(which, copies, out):
        for copy in copies:
            copy.wait()
        for half in range(2):
            for part in range(2):
                i = (1 - half) * 2 + 1 - part
                for level in range(2):
                    out[level, pl.ds(half * 3, 3), pl.ds(part * HALF, HALF)] = ex_r[
                        which, i, pl.ds(level * 3, 3), :
                    ].astype(BF16)

    arrive(0, exit_block, o_block)
    arrive(1, exit_token, o_token)

    for copy in copies_5:
        copy.wait()
    copies_6 = [push(fin.at[mine], fin.at[mine], s_6, j - 1, at_x(j)) for j in range(1, nx)]
    for copy in copies_b3:
        copy.wait()
    flat = b_fin[...].reshape(256, 128).astype(F32)
    for h in range(HEADS):
        o_bias[0, h, :, 0:128] = flat[h * 24 : h * 24 + 23]
        o_bias[0, h, :, 128:144] = flat[144:167, h * 16 : h * 16 + 16]
    for copy in copies_6:
        copy.wait()
    ours = fin.at[pl.ds(core * nx, nx)]
    push(ours, ours, s_7, 0, at_core()).wait()

    scale = float(cells) ** (-0.5)

    def take(per, base, start, rows):
        parts = [
            fin[piece, pl.ds(base + row, count), :]
            for _, piece, row, count in flat_pieces(per, start, rows)
        ]
        whole = parts[0] if len(parts) == 1 else jnp.concatenate(parts, axis=0)
        return whole.astype(F32) * scale

    for i in range(6):
        o_up[:, pl.ds(i * 128, 128)] = take(ra, 0, i * 192, 192)
    o_down[:, 0:128] = take(ra, 0, 1152, 768)
    rest = take(ra, 0, 1920, 384)
    o_down[0:384, 128:192] = rest[:, :64]
    o_down[384:768, 128:192] = rest[:, 64:]
    for i in range(4):
        o_qkv[:, pl.ds(i * 128, 128)] = take(rc, ra, i * 192, 192)
    o_proj[:, 0:128] = take(rc, ra, 768, 192)
    rest = take(rc, ra, 960, 192)
    o_qkv[:, 512:576] = rest[:, :64]
    o_proj[:, 128:192] = rest[:, 64:]
    rest = take(rc, ra, 1152, 16)
    o_n1[:, 0:128] = rest[0:1, :]
    o_n1[:, 128:192] = rest[1:2, :64]
    o_n2[:, 0:128] = rest[2:3, :]
    o_n2[:, 128:192] = rest[3:4, :64]


def on_device(geo, tokens, labels, gain1, wqkv, wproj, table, gain2, wup, wdown, cotangent):
    nlat, nlon, ny_lo, nx, nz, ny_hi = geo
    ny = ny_lo * ny_hi
    pieces = 2 * nx
    ra, rc = ROWS_A // pieces, ROWS_C // pieces
    ry = (ra + rc) // ny
    rb = 256 // nz
    vmem = pltpu.VMEM
    scratch = [
        vmem((4, 16, HALF), F32),
        vmem((3, 16, HALF), BF16),
        vmem((3, 16, HALF), BF16),
        vmem((192, C), F32),
        vmem((192, C), F32),
        vmem((16, 128), F32),
        vmem((368, 192), F32),
        vmem((HEADS, 192, 192), F32),
        vmem((HEADS, 192, 192), F32),
        vmem((2, 4, 8, HALF), F32),
        vmem((2, 4, 8, HALF), F32),
        vmem((192, C), F32),
        vmem((pieces, ra, 128), BF16),
        vmem((pieces, rc, 128), BF16),
        vmem((nx, ra, 128), BF16),
        vmem((nx, rc, 128), BF16),
        vmem((nx, ra, 128), BF16),
        vmem((nx, rc, 128), BF16),
        vmem((nx - 1, ra, 128), BF16),
        vmem((nx - 1, rc, 128), BF16),
        vmem((ra + rc, 128), BF16),
        vmem((ny - 1, ry, 128), BF16),
        vmem((nz, ry, 128), BF16),
        vmem((pieces, ra + rc, 128), BF16),
        vmem((16, 128), F32),
        vmem((HEADS, 192, 192), BF16),
        vmem((368, 192), BF16),
        vmem((256, 128), F32),
        vmem((nz, rb, 128), BF16),
        vmem((nz - 1, rb, 128), BF16),
        vmem((ny_hi, rb, 128), BF16),
        vmem((nz, rb, 128), BF16),
    ]
    for count in (3, 3, 3, 1, 1, nx - 1, nx - 1, ny - 1, nz - 1, ny - 1, nx - 1, 1, nz - 1, ny_hi - 1, nz - 1):
        scratch += [pltpu.SemaphoreType.DMA((count,)), pltpu.SemaphoreType.DMA((count,))]
    shape = jax.ShapeDtypeStruct
    whole = pl.BlockSpec(memory_space=vmem)
    out = pl.pallas_call(
        functools.partial(kernel, geo),
        out_shape=(
            shape(tokens.shape, BF16),
            shape(tokens.shape, BF16),
            shape((1, C), F32),
            shape((C, 3 * C), F32),
            shape((C, C), F32),
            shape(table.shape, F32),
            shape((1, C), F32),
            shape((C, FFN), F32),
            shape((FFN, C), F32),
        ),
        in_specs=[whole] * 10,
        out_specs=(whole,) * 9,
        scratch_shapes=scratch,
        compiler_params=pltpu.CompilerParams(
            collective_id=0, has_side_effects=True, vmem_limit_bytes=48 * 1024 * 1024
        ),
    )(
        tokens, labels, gain1.reshape(1, C), wqkv, wproj, table, gain2.reshape(1, C), wup, wdown,
        cotangent,
    )
    out = list(out)
    out[2] = out[2].reshape(C)
    out[6] = out[6].reshape(C)
    return tuple(out)


def geometry(mesh):
    nlat, nlon = mesh.shape["lat"], mesh.shape["lon"]
    ny_hi = 4 if nlon == 32 else 2
    nx = min(4, nlat // 2)
    return nlat, nlon, nlat // 2 // nx, nx, nlon // ny_hi, ny_hi


def solution(mesh):
    cells, band = P(None, "lat", "lon"), P("lat", None, None, None)
    return jax.shard_map(
        functools.partial(on_device, geometry(mesh)),
        mesh=mesh,
        in_specs=(cells, cells, P(), P(), P(), band, P(), P(), P(), cells),
        out_specs=(cells, cells, P(), P(), P(), band, P(), P(), P()),
        check_vma=False,
    )
```

time: 512 us -> 73.2 us (0.14)
  blocking collectives: 223 us -> 0 us
  waiting for transfers between devices: 149 us -> 0 us
  Pallas kernels: 0 us -> 61.2 us
  starting transfers between devices: 40 us -> 0 us
  local copies, waits for them, and re-layouts: 44.7 us -> 11 us
  matrix products: 23.4 us -> 0 us
  other arithmetic: 14.6 us -> 0 us
  between operations: 14.6 us -> 0.73 us
    psum x2 -> x0, blocking collectives: 223 us -> none  [the longest x1 126 us: on_device(): lax.psum(bias_grad.astype(jnp.bfloat16), 'lon').astype(jnp.float32)]
    psum x1 -> x0, waiting for transfers between devices: 144 us -> none  [on_device(): lax.psum((gain_one, qkv_grad, proj_grad, gain_two, up_grad, down_grad), (...]
    pallas_call x0 -> x1, Pallas kernels: none -> 61.2 us  [on_device(): pl.pallas_call(functools.partial(kernel, geo), out_shape=(shape(tokens.sh...]
    ppermute x8 -> x0, starting transfers between devices: 40 us -> none  [shifted(): return lax.ppermute(block, axis, route)]
    dot_general x20 -> x0, matrix products: 23.4 us -> none  [the longest x1 5.03 us: expand_bias(): jnp.einsum('hdp,ed->hpe', table_band, lon_table(), precision=lax.Precisio...]
    reshape x8 -> x0, local copies, waits for them, and re-layouts: 22.5 us -> none  [the longest x2 16.3 us: attend(): scores = scores * head_size ** (-0.5) + expand_bias(table_band)[None]]
    mul x7 -> x0, other arithmetic: 9.28 us -> none  [the longest x1 1.93 us: on_device(): totals[4] * grad_scale]
    transpose x1 -> x0, local copies, waits for them, and re-layouts: 8.4 us -> none  [fold_bias(): grad_full.reshape(head_count, 2, 6, 12, 2, 6, 12)]
  transfers between devices with their start and end apart: 9 -> 0, of which waited for: 4 -> 0; matrix products, arithmetic and copies ran while one was open for 11% -> 0% of each run, Pallas kernels for 0% -> 0%
where the time goes in v1:
time: 73.2 us; the launch traced here: 72.9 us
  Pallas kernels  61.2 us (84%)
  local copies, waits for them, and re-layouts  11 us (15%)
    pallas_call x1, Pallas kernels, on_device(): pl.pallas_call(functools.partial(kernel, geo), out_shape=(shape(tokens.sh...  61.2 us
    unnamed x26, local copies, waits for them, and re-layouts  11 us

profile of v1, /device:TPU:1, one launch (start us, length us, event | category | flops | bytes accessed | tf_op | source)
XLA Modules:
  0.0 72.9 jit_solution(14500939679248865988)
XLA Ops:
  0.6 0.0 copy-start.5
  0.7 0.7 %copy.20.lab = s32[2,6,12]{2,1,0:T(8,128)S(1)} copy(s32[2,6,12]{2,0,1:T(2,128)} %param.11) | data formatting | bytes 1152 | tf_op args[1]
  1.4 0.8 %copy.19.tok = bf16[2,6,2304]{2,1,0:T(8,128)(2,1)S(1)} copy(bf16[2,6,2304]{2,0,1:T(2,128)(2,1)} %param.10) | data formatting | bytes 110592 | tf_op args[0]
  2.2 0.8 %copy.23.cot = bf16[2,6,2304]{2,1,0:T(8,128)(2,1)S(1)} copy(bf16[2,6,2304]{2,0,1:T(2,128)(2,1)} %param.19) | data formatting | bytes 110592 | tf_op args[9]
  3.0 0.9 %copy.21.btab = f32[1,6,23,144]{3,2,1,0:T(8,128)S(1)} copy(f32[1,6,23,144]{3,0,2,1:T(1,128)} %param.15) | data formatting | bytes 158976 | tf_op args[5]
  4.0 0.0 copy-start
  4.0 0.0 copy-start.1
  4.0 0.0 copy-start.2
  4.0 0.0 copy-start.3
  4.0 0.0 copy-start.4
  4.0 0.2 copy.22.wdown
  4.2 0.7 %copy-done = bf16[192,768]{1,0:T(8,128)(2,1)S(1)} copy-done((bf16[192,768]{1,0:T(8,128)(2,1)S(1)}, bf16[192,768]{1,0:T(8,128)(2,1)}, u32[]{:S(2)}) %copy-start) | copy-done | bytes 294936
  4.9 0.1 copy-done.1
  5.0 0.1 copy-done.2
  5.1 61.2 %shard_map.169 = (bf16[2,6,2304]{2,1,0:T(8,128)(2,1)S(1)}, bf16[2,6,2304]{2,1,0:T(8,128)(2,1)S(1)}, f32[1,192]{1,0:T(1,128)S(1)}, f32[192,576]{1,0:T(8,128)S(1)}...) custom-call(bf16[2,6,2304]{2,1,0:T(8,128)(2,1)S(1)} %copy.19.tok, ...), custom_call_target="tpu_custom_call" | custom-call | tf_op jit(solution)/shard_map/pallas_call | solution.py:500
  66.3 0.7 copy.24
  67.0 0.7 copy.25
  67.7 0.8 %copy.26 = f32[1,6,23,144]{3,0,2,1:T(1,128)} copy(f32[1,6,23,144]{3,2,1,0:T(8,128)S(1)} %get-tuple-element.32) | data formatting | bytes 158976
  68.5 1.1 %copy.27 = f32[768,192]{0,1:T(8,128)} copy(f32[768,192]{1,0:T(8,128)S(1)} %get-tuple-element.35) | data formatting | bytes 1179648
  69.5 0.6 copy.33
  70.1 0.8 %copy.34 = f32[192,576]{1,0:T(8,128)} copy(f32[192,576]{1,0:T(8,128)S(1)} %get-tuple-element.48) | data formatting | bytes 884736
  70.9 0.7 copy.35
  71.5 0.6 copy.36
  72.1 0.8 %copy.37 = f32[192,768]{1,0:T(8,128)} copy(f32[192,768]{1,0:T(8,128)S(1)} %get-tuple-element.52) | data formatting | bytes 1179648
  (3 shorter events, 0.0 us)
Async XLA Ops:
  0.6 3.3 %copy-start.5 = (bf16[768,192]{0,1:T(8,128)(2,1)S(1)}, bf16[768,192]{0,1:T(8,128)(2,1)}, u32[]{:S(2)}) copy-start(bf16[768,192]{0,1:T(8,128)(2,1)} %param.18) | copy-start | bytes 884740
  4.0 1.0 %copy-start = (bf16[192,768]{1,0:T(8,128)(2,1)S(1)}, bf16[192,768]{1,0:T(8,128)(2,1)}, u32[]{:S(2)}) copy-start(bf16[192,768]{1,0:T(8,128)(2,1)} %wup.1) | copy-start | bytes 884740
  4.0 1.0 %copy-start.1 = (bf16[192,576]{1,0:T(8,128)(2,1)S(1)}, bf16[192,576]{1,0:T(8,128)(2,1)}, u32[]{:S(2)}) copy-start(bf16[192,576]{1,0:T(8,128)(2,1)} %wqkv.1) | copy-start | bytes 663556
  4.0 1.1 %copy-start.2 = (bf16[192,192]{1,0:T(8,128)(2,1)S(1)}, bf16[192,192]{1,0:T(8,128)(2,1)}, u32[]{:S(2)}) copy-start(bf16[192,192]{1,0:T(8,128)(2,1)} %wproj.1) | copy-start | bytes 221188
  4.0 1.1 %copy-start.3 = (f32[192]{0:T(256)S(1)}, f32[192]{0:T(256)}, u32[]{:S(2)}) copy-start(f32[192]{0:T(256)} %param.12) | copy-start | bytes 2308
  4.0 1.1 %copy-start.4 = (f32[192]{0:T(256)S(1)}, f32[192]{0:T(256)}, u32[]{:S(2)}) copy-start(f32[192]{0:T(256)} %param.16) | copy-start | bytes 2308

commit v2 on v1

v2 whole, which is shorter than its diff:
```python
import functools

import jax
import jax.numpy as jnp
from jax import lax
from jax.experimental import pallas as pl
from jax.experimental.pallas import tpu as pltpu
from jax.sharding import PartitionSpec as P

MESH = pl.DeviceIdType.MESH
F32, BF16 = jnp.float32, jnp.bfloat16
C, HEADS, FFN = 192, 6, 768
HALF = 6 * C
EPS = 1e-05
COEFF = 0.044715
ROOT = 0.7978845608028654
MASKED = -1e30
SCALE = 32.0**-0.5
ROWS = (2048, 768, 768)


def nn(a, b):
    return jnp.dot(a, b, preferred_element_type=F32)


def nt(a, b):
    return lax.dot_general(a, b, (((1,), (1,)), ((), ())), preferred_element_type=F32)


def tn(a, b):
    return lax.dot_general(a, b, (((0,), (0,)), ((), ())), preferred_element_type=F32)


def mean(x):
    return jnp.sum(x, axis=-1, keepdims=True) * (1.0 / C)


def norm(x, gain):
    center = x - mean(x)
    inv = lax.rsqrt(mean(center * center) + EPS)
    xhat = center * inv
    return (xhat * gain).astype(BF16), xhat, inv


def norm_back(grad, xhat, inv, gain):
    g = grad * gain
    grad_in = inv * (g - mean(g) - xhat * mean(g * xhat))
    return grad_in, jnp.sum(grad * xhat, axis=0, keepdims=True)


def iota(shape, dim):
    return lax.broadcasted_iota(jnp.int32, shape, dim)


def cell_row(rho):
    half, r = rho >> 3, rho & 7
    return (r & 1) * 6 + half * 3 + (r >> 1), r < 6


def flat_pieces(sizes, start, rows):
    at = start
    while at < start + rows:
        group, base = 0, 0
        while at >= base + ROWS[group]:
            base += ROWS[group]
            group += 1
        per = sizes[group]
        inside = at - base
        take = min(per - inside % per, start + rows - at)
        yield at - start, group, inside // per, inside % per, take
        at += take


def kernel(
    geo, *refs,
):
    inputs, outs, held, ready, refs = refs[:10], refs[10:19], refs[19:29], refs[29:38], refs[38:]
    tok, lab, g1, wqkv, wproj, btab, g2, wup, wdown, cot = held
    o_block, o_token, o_n1, o_qkv, o_proj, o_bias, o_n2, o_up, o_down = ready
    (
        stage, ent_s, ent_r, xs, gs, labs, ytab, bias, probs, ex_s, ex_r, rows_st,
        nst, zfold, ffold, fsum, bst, b_s, b_r1, b_y, b_fin,
        buf_a, c_a, m1_a, r2_a, m2_a, r3_a, z_a, fin_a,
        buf_b, c_b, m1_b, r2_b, x_b, z_b, fin_b,
        buf_d, c_d, m1_d, r2_d, x_d, z_d, fin_d,
    ) = refs[:43]
    in_sem, out_sem, *sems = refs[43:]
    loads = {}
    for i in (0, 9, 1, 5, 2, 3, 4, 6, 7, 8):
        loads[i] = pltpu.make_async_copy(inputs[i], held[i], in_sem.at[i])
        loads[i].start()
    nlat, nlon, ny_lo, nx, nz, ny_hi = geo
    ny = ny_lo * ny_hi
    per = piece_rows(geo)
    bufs, fins = (buf_a, buf_b, buf_d), (fin_a, fin_b, fin_d)
    cells = 144 * nlat * nlon
    s_ent, s_exb, s_ext, s_b1, s_b2, s_b3, *s_groups = [
        (sems[2 * i], sems[2 * i + 1]) for i in range(len(sems) // 2)
    ]
    s_a, s_b, s_d = s_groups[:7], s_groups[7:13], s_groups[13:19]

    lat, lon = lax.axis_index("lat"), lax.axis_index("lon")
    core = lax.rem(lat, 2)
    x = lax.rem(lat // 2, nx)
    y_lo = lat // (2 * nx)
    z = lon // ny_hi
    y_hi = lax.rem(lon, ny_hi)
    y = y_hi * ny_lo + y_lo

    def at_core():
        return (lat + 1 - 2 * core, lon)

    def at_x(k):
        return ((y_lo * nx + lax.rem(x + k, nx)) * 2 + core, lon)

    def at_y(k):
        other = lax.rem(y + k, ny)
        return ((lax.rem(other, ny_lo) * nx + x) * 2 + core, z * ny_hi + other // ny_lo)

    def at_yhi(k):
        return (lat, z * ny_hi + lax.rem(y_hi + k, ny_hi))

    def at_z(k):
        return (lat, lax.rem(z + k, nz) * ny_hi + y_hi)

    def near(da, db):
        return (lax.rem(lat + da + nlat, nlat), lax.rem(lon + db + nlon, nlon))

    def push(src, dst, sem, i, dev):
        copy = pltpu.make_async_remote_copy(
            src_ref=src, dst_ref=dst, send_sem=sem[0].at[i], recv_sem=sem[1].at[i],
            device_id=dev, device_id_type=MESH,
        )
        copy.start()
        return copy

    barrier = pltpu.get_barrier_semaphore()
    partners = [at_core()]
    partners += [at_x(k) for k in range(1, nx)]
    partners += [at_y(k) for k in range(1, ny)]
    partners += [at_z(k) for k in range(1, nz)]
    partners += [near(-1, 0), near(0, -1), near(-1, -1), near(1, 0), near(0, 1), near(1, 1)]
    for dev in partners:
        pl.semaphore_signal(barrier, inc=1, device_id=dev, device_id_type=MESH)

    loads[0].wait()
    loads[9].wait()

    stage[...] = jnp.zeros_like(stage)
    for half in range(2):
        for part in range(2):
            for kind, ref in enumerate((tok, cot)):
                for row in range(3):
                    stage[half * 2 + part, pl.ds(kind * 8 + row * 2, 2), :] = ref[
                        half * 3 + row, :, pl.ds(part * HALF, HALF)
                    ].astype(F32)
    for i in range(3):
        ent_s[i] = stage[i].astype(BF16)
    pl.semaphore_wait(barrier, len(partners))
    entry = [
        push(ent_s.at[i], ent_r.at[i], s_ent, i, near(half - 1, part - 1))
        for i, (half, part) in enumerate(((0, 0), (0, 1), (1, 0)))
    ]

    loads[1].wait()
    loads[5].wait()

    labs[...] = jnp.full_like(labs, -1.0)
    for half in range(2):
        for row in range(3):
            labs[pl.ds(half * 8 + row * 2, 2), pl.ds(0, 12)] = lab[half * 3 + row].astype(F32)
    lab16 = labs[...].astype(BF16)
    pick = (11 - (iota((192, 128), 0) >> 4) == iota((192, 128), 1)).astype(F32).astype(BF16)
    lane_all = nt(lab16, pick)
    lane_lab = jnp.sum(
        jnp.where(iota((16, 192), 0) == (iota((16, 192), 1) & 15), lane_all, 0.0),
        axis=0, keepdims=True,
    )
    row_all = nt(pick, lab16)
    row_lab = jnp.sum(
        jnp.where(iota((192, 16), 1) == (iota((192, 16), 0) & 15), row_all, 0.0),
        axis=1, keepdims=True,
    )
    same = row_lab == lane_lab

    place, real = cell_row(iota((16, 144), 0))
    spot = iota((16, 144), 1)
    spot_row = (spot * 171) >> 11
    m1 = jnp.where((spot_row == place) & real, 1.0, 0.0)
    place_j, real_j = cell_row(iota((144, 192), 1) & 15)
    spot_j = iota((144, 192), 0)
    spot_col = spot_j - ((spot_j * 171) >> 11) * 12
    m2 = jnp.where((spot_col == place_j) & real_j, 1.0, 0.0).astype(BF16)
    group = iota((192, 192), 1) >> 4

    def build(h, carry):
        left = btab[h]
        full = jnp.zeros((368, 192), F32)
        for _ in range(3):
            piece = left.astype(BF16).astype(F32)
            left = left - piece
            wide = (piece * m1[None]).reshape(368, 144)
            full = full + nn(wide.astype(BF16), m2)
        ytab[...] = full
        out = ytab[pl.ds(176, 192), :]
        for bj in range(1, 12):
            out = jnp.where(group == bj, ytab[pl.ds((11 - bj) * 16, 192), :], out)
        bias[h] = jnp.where(same, out, MASKED)
        return carry

    lax.fori_loop(0, HEADS, build, 0)
    buf_d[...] = jnp.zeros_like(buf_d)
    nst[...] = jnp.zeros_like(nst)
    bst[...] = jnp.zeros_like(bst)

    def lay(quarter, half, part):
        for c in range(6):
            row = (11 - part * 6 - c) * 16 + half * 8
            xs[pl.ds(row, 8), :] = quarter[0:8, c * C : (c + 1) * C]
            gs[pl.ds(row, 8), :] = quarter[8:16, c * C : (c + 1) * C]

    for i in (2, 3, 4, 6, 7, 8):
        loads[i].wait()
    lay(stage[3], 0, 0)
    for i, (half, part) in enumerate(((1, 1), (1, 0), (0, 1))):
        entry[i].wait()
        lay(ent_r[i].astype(F32), half, part)

    gain1, gain2 = g1[...], g2[...]
    tokens = xs[...]
    n1, xhat1, inv1 = norm(tokens, gain1)
    packed = nn(n1, wqkv[...]).astype(BF16)
    q, k, v = packed[:, :C], packed[:, C : 2 * C], packed[:, 2 * C :]
    head_of = iota((1, C), 1) >> 5
    masks = [(head_of == h).astype(F32).astype(BF16) for h in range(HEADS)]
    mixed = jnp.zeros((192, C), F32)
    for h in range(HEADS):
        s = nt(q * masks[h], k) * SCALE + bias[h]
        e = jnp.exp(s - jnp.max(s, axis=-1, keepdims=True))
        p = e * (1.0 / jnp.sum(e, axis=-1, keepdims=True))
        probs[h] = p
        mixed = mixed + nn(p.astype(BF16), v * masks[h])
    mixed = mixed.astype(BF16)
    branch = nn(mixed, wproj[...]).astype(BF16)
    residual = tokens + branch.astype(F32)
    n2, xhat2, inv2 = norm(residual, gain2)
    pre = nn(n2, wup[...])
    square = pre * pre
    tanh = jnp.tanh(ROOT * (pre + COEFF * pre * square))
    hidden = (0.5 * pre * (1.0 + tanh)).astype(BF16)
    slope = 0.5 * (1.0 + tanh) + 0.5 * pre * (1.0 - tanh * tanh) * ROOT * (
        1.0 + 3.0 * COEFF * square
    )
    block = residual + nt(hidden, wdown[...])

    def leave(which, value, sem):
        rows_st[...] = value
        copies = []
        for half in range(2):
            for part in range(2):
                i = half * 2 + part
                out = ex_r.at[which, 0] if i == 0 else ex_s.at[which, i]
                for c in range(6):
                    row = (11 - part * 6 - c) * 16 + half * 8
                    out[:, pl.ds(c * C, C)] = rows_st[pl.ds(row, 8), :]
                if i:
                    copies.append(
                        push(ex_s.at[which, i], ex_r.at[which, i], sem, i - 1, near(half, part))
                    )
        return copies

    exit_block = leave(0, block, s_exb)

    grads = gs[...]
    grads16 = grads.astype(BF16)
    grad_pre = (nn(grads16, wdown[...]) * slope).astype(BF16)
    down = tn(grads16, hidden)
    up = tn(n2, grad_pre)

    def put(start, value, lanes=(0, 128)):
        value = value.astype(BF16)
        for src, group, piece, row, take in flat_pieces(per, start, value.shape[0]):
            bufs[group][piece, pl.ds(row, take), pl.ds(lanes[0], lanes[1] - lanes[0])] = value[
                src : src + take
            ]

    for i in range(6):
        put(i * 192, up[:, i * 128 : (i + 1) * 128])
        put(1152 + i * 192, down[:, i * 128 : (i + 1) * 128])

    def half_to_core(buf, dst, sem, count):
        return push(buf.at[pl.ds((1 - core) * count, count)], dst, sem, 0, at_core())

    def own_half(buf, other, out, count, copy):
        copy.wait()
        for i in range(count):
            out[i] = (buf[core * count + i].astype(F32) + other[i].astype(F32)).astype(BF16)

    def deal(pieces, slots, sem, me, count, where):
        return [
            push(pieces(lax.rem(me + j, count)), slots.at[j - 1], sem, j - 1, where(j))
            for j in range(1, count)
        ]

    def share(ref, sem, count, where):
        return [push(ref, ref, sem, j - 1, where(j)) for j in range(1, count)]

    def sum_dealt(own, copies, slots):
        total = own.astype(F32)
        for i, copy in enumerate(copies):
            copy.wait()
            total = total + slots[i].astype(F32)
        return total.astype(BF16)

    def sum_shared(copies, slots, count):
        for copy in copies:
            copy.wait()
        total = slots[0].astype(F32)
        for i in range(1, count):
            total = total + slots[i].astype(F32)
        return total.astype(BF16)

    copies_a = half_to_core(buf_a, c_a, s_a[0], nx)

    grad_n2 = nt(grad_pre, wup[...])
    grad_in, norm2 = norm_back(grad_n2, xhat2, inv2, gain2)
    grad_res = grads + grad_in
    grad_branch = grad_res.astype(BF16)
    proj = tn(mixed, grad_branch)
    grad_mixed = nt(grad_branch, wproj[...]).astype(BF16)

    def piece_of(ref, index):
        size = per[0] // ny
        return ref.at[pl.ds(pl.multiple_of(index * size, 16), size)]

    dq = jnp.zeros((192, C), F32)
    dk = jnp.zeros((192, C), F32)
    dv = jnp.zeros((192, C), F32)
    for h in range(HEADS):
        gm = grad_mixed * masks[h]
        p = probs[h]
        dp = nt(gm, v)
        t = p * dp
        ds = ((t - p * jnp.sum(t, axis=-1, keepdims=True)) * SCALE).astype(BF16)
        zfold[h] = ds
        dv = dv + tn(p.astype(BF16), gm)
        dk = dk + tn(ds, q * masks[h])
        dq = dq + nn(ds, k * masks[h])
        if h == 1:
            own_half(buf_a, c_a, m1_a, nx, copies_a)
            copies_a = deal(lambda i: m1_a.at[i], r2_a, s_a[1], x, nx, at_x)
        if h == 5:
            m2_a[...] = sum_dealt(m1_a[x], copies_a, r2_a)
            copies_a = deal(lambda i: piece_of(m2_a, i), r3_a, s_a[2], y, ny, at_y)
    grad_packed = jnp.concatenate([dq, dk, dv], axis=1).astype(BF16)
    qkv = tn(n1, grad_packed)
    grad_n1 = nt(grad_packed, wqkv[...])
    grad_in1, norm1 = norm_back(grad_n1, xhat1, inv1, gain1)

    for i in range(4):
        put(2304 + i * 192, qkv[:, i * 128 : (i + 1) * 128])
    put(3072, proj[:, :128])
    put(3264, qkv[:, 512:], (0, 64))
    put(3264, proj[:, 128:], (64, 128))
    nst[0:1, :] = norm1[:, :128]
    nst[1:2, 0:64] = norm1[:, 128:]
    nst[2:3, :] = norm2[:, :128]
    nst[3:4, 0:64] = norm2[:, 128:]
    put(3456, nst[...])
    copies_b = half_to_core(buf_b, c_b, s_b[0], ny)
    copies_d = half_to_core(buf_d, c_d, s_d[0], nz)

    token_grad = grad_res + grad_in1.astype(BF16).astype(F32)
    exit_token = leave(1, token_grad, s_ext)

    z_a[z] = sum_dealt(piece_of(m2_a, y)[...], copies_a, r3_a)
    copies_a = share(z_a.at[z], s_a[3], nz, at_z)
    own_half(buf_b, c_b, m1_b, ny, copies_b)
    copies_b = deal(lambda i: m1_b.at[i], r2_b, s_b[1], y, ny, at_y)
    own_half(buf_d, c_d, m1_d, nz, copies_d)
    copies_d = deal(lambda i: m1_d.at[i], r2_d, s_d[1], z, nz, at_z)

    def fold(h, carry):
        ds = zfold[h]
        ffold[...] = jnp.zeros_like(ffold)
        for bj in range(12):
            one = (iota((1, 192), 1) >> 4 == bj).astype(F32).astype(BF16)
            ffold[pl.ds((11 - bj) * 16, 192), :] += ds * one
        wide = nt(ffold[...], m2).reshape(23, 16, 144) * m1[None]
        fsum[h, 0:23, :] = jnp.sum(wide, axis=1) * (1.0 / SCALE)
        return carry

    lax.fori_loop(0, HEADS, fold, 0)
    for h in range(HEADS):
        bst[pl.ds(h * 24, 23), :] = fsum[h, 0:23, 0:128]
        bst[pl.ds(144, 23), pl.ds(h * 16, 16)] = fsum[h, 0:23, 128:144]
    rb = 256 // nz
    b_s[...] = bst[...].astype(BF16).reshape(nz, rb, 128)
    copies_bias = deal(lambda i: b_s.at[i], b_r1, s_b1, z, nz, at_z)

    mine = core * nx + x
    done = piece_of(fin_a.at[mine], y)
    done[...] = sum_shared(copies_a, z_a, nz)
    copies_a = share(done, s_a[4], ny, at_y)
    x_b[x] = sum_dealt(m1_b[y], copies_b, r2_b)
    copies_b = share(x_b.at[x], s_b[2], nx, at_x)
    x_d[x] = sum_dealt(m1_d[z], copies_d, r2_d)
    copies_d = share(x_d.at[x], s_d[2], nx, at_x)
    b_y[y_hi] = sum_dealt(b_s[z], copies_bias, b_r1)
    copies_bias = share(b_y.at[y_hi], s_b2, ny_hi, at_yhi)

    for copy in copies_a:
        copy.wait()
    copies_a = share(fin_a.at[mine], s_a[5], nx, at_x)
    passed_a = [push(fin_a.at[mine], fin_a.at[mine], s_a[6], 0, at_core())]
    z_b[z] = sum_shared(copies_b, x_b, nx)
    copies_b = share(z_b.at[z], s_b[3], nz, at_z)
    z_d[y] = sum_shared(copies_d, x_d, nx)
    copies_d = share(z_d.at[y], s_d[3], ny, at_y)
    b_fin[z] = sum_shared(copies_bias, b_y, ny_hi)
    copies_bias = share(b_fin.at[z], s_b3, nz, at_z)

    def pass_on(fin, copies, sem, me, count):
        passed = []
        for j, copy in enumerate(copies, 1):
            copy.wait()
            got = fin.at[core * count + lax.rem(me - j + count, count)]
            passed.append(push(got, got, sem, j, at_core()))
        return passed

    def finish(copies, sem, fin, me, slots, count, others, where):
        own = fin.at[core * count + me]
        own[...] = sum_shared(copies, slots, others)
        passed = [push(own, own, sem[5], 0, at_core())]
        return share(own, sem[4], count, where), passed

    copies_b, passed_b = finish(copies_b, s_b, fin_b, y, z_b, ny, nz, at_y)
    copies_d, passed_d = finish(copies_d, s_d, fin_d, z, z_d, nz, ny, at_z)
    passed_a += pass_on(fin_a, copies_a, s_a[6], x, nx)

    stores = []

    def store(*which):
        for i in which:
            copy = pltpu.make_async_copy(ready[i], outs[i], out_sem.at[i])
            copy.start()
            stores.append(copy)

    def arrive(which, copies, out):
        for copy in copies:
            copy.wait()
        for half in range(2):
            for part in range(2):
                i = (1 - half) * 2 + 1 - part
                for row in range(3):
                    out[half * 3 + row, :, pl.ds(part * HALF, HALF)] = ex_r[
                        which, i, pl.ds(row * 2, 2), :
                    ].astype(BF16)

    arrive(0, exit_block, o_block)
    arrive(1, exit_token, o_token)

    store(0, 1)
    for copy in copies_bias:
        copy.wait()
    flat = b_fin[...].reshape(256, 128).astype(F32)
    for h in range(HEADS):
        o_bias[h, :, 0, 0:128] = flat[h * 24 : h * 24 + 23]
        o_bias[h, :, 0, 128:144] = flat[144:167, h * 16 : h * 16 + 16]
    store(5)
    passed_b += pass_on(fin_b, copies_b, s_b[5], y, ny)
    passed_d += pass_on(fin_d, copies_d, s_d[5], z, nz)

    scale = float(cells) ** (-0.5)

    def take(start, rows):
        parts = [
            fins[group][piece, pl.ds(row, count), :]
            for _, group, piece, row, count in flat_pieces(per, start, rows)
        ]
        whole = parts[0] if len(parts) == 1 else jnp.concatenate(parts, axis=0)
        return whole.astype(F32) * scale

    for copy in passed_a:
        copy.wait()
    for i in range(6):
        o_up[:, pl.ds(i * 128, 128)] = take(i * 192, 192)
    store(7)
    for copy in passed_b:
        copy.wait()
    for i in range(6):
        o_down[:, pl.ds(i * 128, 128)] = take(1152 + i * 192, 192)
    store(8)
    for copy in passed_d:
        copy.wait()
    for i in range(4):
        o_qkv[:, pl.ds(i * 128, 128)] = take(2304 + i * 192, 192)
    o_proj[:, 0:128] = take(3072, 192)
    rest = take(3264, 192)
    o_qkv[:, 512:576] = rest[:, :64]
    o_proj[:, 128:192] = rest[:, 64:]
    rest = take(3456, 16)
    o_n1[:, 0:128] = rest[0:1, :]
    o_n1[:, 128:192] = rest[1:2, :64]
    o_n2[:, 0:128] = rest[2:3, :]
    o_n2[:, 128:192] = rest[3:4, :64]
    store(2, 3, 4, 6)
    for copy in stores:
        copy.wait()


def piece_rows(geo):
    nlat, nlon, ny_lo, nx, nz, ny_hi = geo
    return ROWS[0] // (2 * nx), ROWS[1] // (2 * ny_lo * ny_hi), ROWS[2] // (2 * nz)


def spread(*refs):
    inputs, outs, held = refs[:9], refs[9:18], refs[18:27]
    sem_in, sem_out = refs[27:]
    order = (7, 8, 3, 5, 4, 0, 1, 2, 6)
    loads = [pltpu.make_async_copy(inputs[i], held[i], sem_in.at[i]) for i in range(9)]
    stores = [pltpu.make_async_copy(held[i], outs[i], sem_out.at[i]) for i in range(9)]
    for i in order:
        loads[i].start()
    for i in order:
        loads[i].wait()
        stores[i].start()
    for i in order:
        stores[i].wait()


def on_device(geo, tokens, labels, gain1, wqkv, wproj, table, gain2, wup, wdown, cotangent):
    nlat, nlon, ny_lo, nx, nz, ny_hi = geo
    ny = ny_lo * ny_hi
    pa, pb, pd = piece_rows(geo)
    rb = 256 // nz
    vmem = pltpu.VMEM
    args = (
        tokens.transpose(1, 0, 2), labels.transpose(1, 0, 2), gain1.reshape(1, C), wqkv, wproj,
        table.transpose(1, 2, 0, 3), gain2.reshape(1, C), wup, wdown.T, cotangent.transpose(1, 0, 2),
    )
    shape = jax.ShapeDtypeStruct
    shapes = (
        shape((6, 2, 12 * C), BF16),
        shape((6, 2, 12 * C), BF16),
        shape((1, C), F32),
        shape((C, 3 * C), F32),
        shape((C, C), F32),
        shape((HEADS, 23, 1, 144), F32),
        shape((1, C), F32),
        shape((C, FFN), F32),
        shape((C, FFN), F32),
    )
    scratch = [vmem(arg.shape, arg.dtype) for arg in args + shapes]
    scratch += [
        vmem((4, 16, HALF), F32),
        vmem((3, 16, HALF), BF16),
        vmem((3, 16, HALF), BF16),
        vmem((192, C), F32),
        vmem((192, C), F32),
        vmem((16, 128), F32),
        vmem((368, 192), F32),
        vmem((HEADS, 192, 192), F32),
        vmem((HEADS, 192, 192), F32),
        vmem((2, 4, 8, HALF), F32),
        vmem((2, 4, 8, HALF), F32),
        vmem((192, C), F32),
        vmem((16, 128), F32),
        vmem((HEADS, 192, 192), BF16),
        vmem((368, 192), BF16),
        vmem((HEADS, 24, 144), F32),
        vmem((256, 128), F32),
        vmem((nz, rb, 128), BF16),
        vmem((nz - 1, rb, 128), BF16),
        vmem((ny_hi, rb, 128), BF16),
        vmem((nz, rb, 128), BF16),
        vmem((2 * nx, pa, 128), BF16),
        vmem((nx, pa, 128), BF16),
        vmem((nx, pa, 128), BF16),
        vmem((nx - 1, pa, 128), BF16),
        vmem((pa, 128), BF16),
        vmem((ny - 1, pa // ny, 128), BF16),
        vmem((nz, pa // ny, 128), BF16),
        vmem((2 * nx, pa, 128), BF16),
    ]
    for first, piece, last in ((ny, pb, nz), (nz, pd, ny)):
        scratch += [
            vmem((2 * first, piece, 128), BF16),
            vmem((first, piece, 128), BF16),
            vmem((first, piece, 128), BF16),
            vmem((first - 1, piece, 128), BF16),
            vmem((nx, piece, 128), BF16),
            vmem((last, piece, 128), BF16),
            vmem((2 * first, piece, 128), BF16),
        ]
    scratch += [
        pltpu.SemaphoreType.DMA((10,)),
        pltpu.SemaphoreType.DMA((9,)),
    ]
    counts = [3, 3, 3, nz - 1, ny_hi - 1, nz - 1]
    counts += [1, nx - 1, ny - 1, nz - 1, ny - 1, nx - 1, nx]
    counts += [1, ny - 1, nx - 1, nz - 1, ny - 1, ny]
    counts += [1, nz - 1, nx - 1, ny - 1, nz - 1, nz]
    for count in counts:
        scratch += [pltpu.SemaphoreType.DMA((count,)), pltpu.SemaphoreType.DMA((count,))]
    anywhere = pl.BlockSpec(memory_space=pl.ANY)
    out = pl.pallas_call(
        functools.partial(kernel, geo),
        out_shape=shapes,
        in_specs=[anywhere] * 10,
        out_specs=(anywhere,) * 9,
        scratch_shapes=scratch,
        compiler_params=pltpu.CompilerParams(
            collective_id=0, has_side_effects=True, vmem_limit_bytes=63 * 1024 * 1024
        ),
    )(*args)
    out = pl.pallas_call(
        spread,
        out_shape=shapes,
        in_specs=[anywhere] * 9,
        out_specs=(anywhere,) * 9,
        scratch_shapes=[vmem(each.shape, each.dtype) for each in shapes]
        + [pltpu.SemaphoreType.DMA((9,)), pltpu.SemaphoreType.DMA((9,))],
        compiler_params=pltpu.CompilerParams(vmem_limit_bytes=63 * 1024 * 1024),
    )(*out)
    block, token, norm1, qkv, proj, bias, norm2, up, down = out
    return (
        block.transpose(1, 0, 2), token.transpose(1, 0, 2), norm1.reshape(C), qkv, proj,
        bias.transpose(2, 0, 1, 3), norm2.reshape(C), up, down.T,
    )


def geometry(mesh):
    nlat, nlon = mesh.shape["lat"], mesh.shape["lon"]
    ny_hi = 4 if nlon == 32 else 2
    nx = min(4, nlat // 2)
    return nlat, nlon, nlat // 2 // nx, nx, nlon // ny_hi, ny_hi


def solution(mesh):
    cells, band = P(None, "lat", "lon"), P("lat", None, None, None)
    return jax.shard_map(
        functools.partial(on_device, geometry(mesh)),
        mesh=mesh,
        in_specs=(cells, cells, P(), P(), P(), band, P(), P(), P(), cells),
        out_specs=(cells, cells, P(), P(), P(), band, P(), P(), P()),
        check_vma=False,
    )
```

time: 73.2 us -> 66.7 us (0.911)
  local copies, waits for them, and re-layouts: 11 us -> 0 us
  Pallas kernels: 61.2 us -> 65.9 us
    unnamed x26 -> x0, local copies, waits for them, and re-layouts: 11 us -> none
    pallas_call x1 -> x2, Pallas kernels: 61.2 us -> 65.9 us  [the longest x1 63.4 us: on_device(): pl.pallas_call(functools.partial(kernel, geo), out_shape=shapes, in_specs...]
where the time goes in v2:
time: 66.7 us; the launch traced here: 66.6 us
  Pallas kernels  65.9 us (99%)
    pallas_call x1, Pallas kernels, on_device(): pl.pallas_call(functools.partial(kernel, geo), out_shape=shapes, in_specs...  63.4 us
    pallas_call x1, Pallas kernels, on_device(): pl.pallas_call(spread, out_shape=shapes, in_specs=[anywhere] * 9, out_spe...  2.54 us

profile of v2, /device:TPU:1, one launch (start us, length us, event | category | flops | bytes accessed | tf_op | source)
XLA Modules:
  0.0 66.6 jit_solution(5433177880291119724)
XLA Ops:
  0.6 63.4 %shard_map.169 = (bf16[6,2,2304]{2,1,0:T(2,128)(2,1)}, bf16[6,2,2304]{2,1,0:T(2,128)(2,1)}, f32[1,192]{1,0:T(1,128)}, f32[192,576]{1,0:T(8,128)}, f32[192,192]{1...) custom-call(bf16[6,2,2304]{2,1,0:T(2,128)(2,1)} %bitcast.15, ...), custom_call_target="tpu_custom_call" | custom-call | tf_op jit(solution)/shard_map/pallas_call | solution.py:607
  64.0 2.5 %shard_map.170 = (bf16[6,2,2304]{2,1,0:T(2,128)(2,1)}, bf16[6,2,2304]{2,1,0:T(2,128)(2,1)}, f32[1,192]{1,0:T(1,128)}, f32[192,576]{1,0:T(8,128)}, f32[192,192]{1...) custom-call(bf16[6,2,2304]{2,1,0:T(2,128)(2,1)} %get-tuple-element.27.refs_, ...), custom_call_target="tpu_custom_call" | custom-call | tf_op jit(solution)/shard_map/pallas_call | solution.py:617

commit v3 on v2

--- a/solution.py
+++ b/solution.py
@@ -16,7 +16,9 @@
 ROOT = 0.7978845608028654
 MASKED = -1e30
 SCALE = 32.0**-0.5
-ROWS = (2048, 768, 768)
+ROWS = (1024, 768, 768, 512, 512)
+AT_UP, AT_DOWN, AT_PROJ, AT_QKV, AT_REST, AT_NORMS = 0, 1152, 2304, 2560, 3328, 3520
+HOLD = 640
 
 
 def nn(a, b):
@@ -80,11 +82,9 @@
     (
         stage, ent_s, ent_r, xs, gs, labs, ytab, bias, probs, ex_s, ex_r, rows_st,
         nst, zfold, ffold, fsum, bst, b_s, b_r1, b_y, b_fin,
-        buf_a, c_a, m1_a, r2_a, m2_a, r3_a, z_a, fin_a,
-        buf_b, c_b, m1_b, r2_b, x_b, z_b, fin_b,
-        buf_d, c_d, m1_d, r2_d, x_d, z_d, fin_d,
-    ) = refs[:43]
-    in_sem, out_sem, *sems = refs[43:]
+        buf_a, c_a, m1_a, r2_a, m2_a, r3_a, z_a, fin_a, *flat_refs,
+    ) = refs[:57]
+    in_sem, out_sem, *sems = refs[57:]
     loads = {}
     for i in (0, 9, 1, 5, 2, 3, 4, 6, 7, 8):
         loads[i] = pltpu.make_async_copy(inputs[i], held[i], in_sem.at[i])
@@ -92,12 +92,14 @@
     nlat, nlon, ny_lo, nx, nz, ny_hi = geo
     ny = ny_lo * ny_hi
     per = piece_rows(geo)
-    bufs, fins = (buf_a, buf_b, buf_d), (fin_a, fin_b, fin_d)
+    flat_refs = [flat_refs[7 * i : 7 * i + 7] for i in range(4)]
+    bufs = (buf_a, *(each[0] for each in flat_refs))
+    fins = (fin_a, *(each[6] for each in flat_refs))
     cells = 144 * nlat * nlon
-    s_ent, s_exb, s_ext, s_b1, s_b2, s_b3, *s_groups = [
+    s_ent, s_ent2, s_exb, s_ext, s_b1, s_b2, s_b3, *s_groups = [
         (sems[2 * i], sems[2 * i + 1]) for i in range(len(sems) // 2)
     ]
-    s_a, s_b, s_d = s_groups[:7], s_groups[7:13], s_groups[13:19]
+    s_a = s_groups[:7]
 
     lat, lon = lax.axis_index("lat"), lax.axis_index("lon")
     core = lax.rem(lat, 2)
@@ -144,23 +146,34 @@
         pl.semaphore_signal(barrier, inc=1, device_id=dev, device_id_type=MESH)
 
     loads[0].wait()
+
+    stage[...] = jnp.zeros_like(stage)
+
+    def quarters(kind, ref):
+        for half in range(2):
+            for part in range(2):
+                for row in range(3):
+                    for side in range(2):
+                        stage[kind, half * 2 + part, pl.ds(side * 8 + row * 2, 2), 0:576] = ref[
+                            half * 3 + row, :, pl.ds(part * HALF + side * 576, 576)
+                        ].astype(F32)
+        for i in range(3):
+            ent_s[kind, i] = stage[kind, i].astype(BF16)
+
+    quarters(0, tok)
+    pl.semaphore_wait(barrier, len(partners))
+    places = ((0, 0), (0, 1), (1, 0))
+
+    def enter(kind, sem):
+        return [
+            push(ent_s.at[kind, i], ent_r.at[kind, i], sem, i, near(half - 1, part - 1))
+            for i, (half, part) in enumerate(places)
+        ]
+
+    entry = enter(0, s_ent)
     loads[9].wait()
-
-    stage[...] = jnp.zeros_like(stage)
-    for half in range(2):
-        for part in range(2):
-            for kind, ref in enumerate((tok, cot)):
-                for row in range(3):
-                    stage[half * 2 + part, pl.ds(kind * 8 + row * 2, 2), :] = ref[
-                        half * 3 + row, :, pl.ds(part * HALF, HALF)
-                    ].astype(F32)
-    for i in range(3):
-        ent_s[i] = stage[i].astype(BF16)
-    pl.semaphore_wait(barrier, len(partners))
-    entry = [
-        push(ent_s.at[i], ent_r.at[i], s_ent, i, near(half - 1, part - 1))
-        for i, (half, part) in enumerate(((0, 0), (0, 1), (1, 0)))
-    ]
+    quarters(1, cot)
+    entry2 = enter(1, s_ent2)
 
     loads[1].wait()
     loads[5].wait()
@@ -209,22 +222,26 @@
         return carry
 
     lax.fori_loop(0, HEADS, build, 0)
-    buf_d[...] = jnp.zeros_like(buf_d)
+    for i in (2, 4):
+        bufs[i][...] = jnp.zeros_like(bufs[i])
     nst[...] = jnp.zeros_like(nst)
     bst[...] = jnp.zeros_like(bst)
 
-    def lay(quarter, half, part):
+    def lay(out, quarter, half, part):
         for c in range(6):
             row = (11 - part * 6 - c) * 16 + half * 8
-            xs[pl.ds(row, 8), :] = quarter[0:8, c * C : (c + 1) * C]
-            gs[pl.ds(row, 8), :] = quarter[8:16, c * C : (c + 1) * C]
+            side, column = c // 3, c % 3
+            out[pl.ds(row, 8), :] = quarter[side * 8 : side * 8 + 8, column * C : (column + 1) * C]
+
+    def land(kind, out, copies):
+        lay(out, stage[kind, 3], 0, 0)
+        for i, (half, part) in enumerate(places):
+            copies[i].wait()
+            lay(out, ent_r[kind, i].astype(F32), 1 - half, 1 - part)
 
     for i in (2, 3, 4, 6, 7, 8):
         loads[i].wait()
-    lay(stage[3], 0, 0)
-    for i, (half, part) in enumerate(((1, 1), (1, 0), (0, 1))):
-        entry[i].wait()
-        lay(ent_r[i].astype(F32), half, part)
+    land(0, xs, entry)
 
     gain1, gain2 = g1[...], g2[...]
     tokens = xs[...]
@@ -271,6 +288,7 @@
 
     exit_block = leave(0, block, s_exb)
 
+    land(1, gs, entry2)
     grads = gs[...]
     grads16 = grads.astype(BF16)
     grad_pre = (nn(grads16, wdown[...]) * slope).astype(BF16)
@@ -283,10 +301,6 @@
             bufs[group][piece, pl.ds(row, take), pl.ds(lanes[0], lanes[1] - lanes[0])] = value[
                 src : src + take
             ]
-
-    for i in range(6):
-        put(i * 192, up[:, i * 128 : (i + 1) * 128])
-        put(1152 + i * 192, down[:, i * 128 : (i + 1) * 128])
 
     def half_to_core(buf, dst, sem, count):
         return push(buf.at[pl.ds((1 - core) * count, count)], dst, sem, 0, at_core())
@@ -320,13 +334,70 @@
             total = total + slots[i].astype(F32)
         return total.astype(BF16)
 
+    def pass_on(fin, copies, sem, me, count):
+        passed = []
+        for j, copy in enumerate(copies, 1):
+            copy.wait()
+            got = fin.at[core * count + lax.rem(me - j + count, count)]
+            passed.append(push(got, got, sem, j, at_core()))
+        return passed
+
+    class Flat:
+        def __init__(self, refs, sem, me, count, where, last, last_count, last_where):
+            self.buf, self.c, self.m1, self.r2, self.x, self.z, self.fin = refs
+            self.sem, self.me, self.count, self.where = sem, me, count, where
+            self.last, self.last_count, self.last_where = last, last_count, last_where
+
+        def start(self):
+            self.copies = half_to_core(self.buf, self.c, self.sem[0], self.count)
+
+        def deal(self):
+            own_half(self.buf, self.c, self.m1, self.count, self.copies)
+            self.copies = deal(
+                lambda i: self.m1.at[i], self.r2, self.sem[1], self.me, self.count, self.where
+            )
+
+        def cross(self):
+            self.x[x] = sum_dealt(self.m1[self.me], self.copies, self.r2)
+            self.copies = share(self.x.at[x], self.sem[2], nx, at_x)
+
+        def far(self):
+            self.z[self.last] = sum_shared(self.copies, self.x, nx)
+            self.copies = share(
+                self.z.at[self.last], self.sem[3], self.last_count, self.last_where
+            )
+
+        def gather(self):
+            own = self.fin.at[core * self.count + self.me]
+            own[...] = sum_shared(self.copies, self.z, self.last_count)
+            self.copies = share(own, self.sem[4], self.count, self.where)
+            self.passed = [push(own, own, self.sem[5], 0, at_core())]
+
+        def pass_on(self):
+            self.passed += pass_on(self.fin, self.copies, self.sem[5], self.me, self.count)
+
+        def wait(self):
+            for copy in self.passed:
+                copy.wait()
+
+    ways = ((y, ny, at_y, z, nz, at_z), (z, nz, at_z, y, ny, at_y))
+    early_y, early_z, late_y, late_z = [
+        Flat(flat_refs[i], s_groups[7 + 6 * i : 13 + 6 * i], *ways[i % 2]) for i in range(4)
+    ]
+
+    for i in range(6):
+        put(AT_UP + i * 192, up[:, i * 128 : (i + 1) * 128])
+        put(AT_DOWN + i * 192, down[:, i * 128 : (i + 1) * 128])
     copies_a = half_to_core(buf_a, c_a, s_a[0], nx)
+    early_y.start()
 
     grad_n2 = nt(grad_pre, wup[...])
     grad_in, norm2 = norm_back(grad_n2, xhat2, inv2, gain2)
     grad_res = grads + grad_in
     grad_branch = grad_res.astype(BF16)
     proj = tn(mixed, grad_branch)
+    put(AT_PROJ, proj[:, :128])
+    early_z.start()
     grad_mixed = nt(grad_branch, wproj[...]).astype(BF16)
 
     def piece_of(ref, index):
@@ -346,9 +417,12 @@
         dv = dv + tn(p.astype(BF16), gm)
         dk = dk + tn(ds, q * masks[h])
         dq = dq + nn(ds, k * masks[h])
-        if h == 1:
+        if h == 0:
             own_half(buf_a, c_a, m1_a, nx, copies_a)
             copies_a = deal(lambda i: m1_a.at[i], r2_a, s_a[1], x, nx, at_x)
+            early_y.deal()
+        if h == 1:
+            early_z.deal()
         if h == 5:
             m2_a[...] = sum_dealt(m1_a[x], copies_a, r2_a)
             copies_a = deal(lambda i: piece_of(m2_a, i), r3_a, s_a[2], y, ny, at_y)
@@ -358,27 +432,24 @@
     grad_in1, norm1 = norm_back(grad_n1, xhat1, inv1, gain1)
 
     for i in range(4):
-        put(2304 + i * 192, qkv[:, i * 128 : (i + 1) * 128])
-    put(3072, proj[:, :128])
-    put(3264, qkv[:, 512:], (0, 64))
-    put(3264, proj[:, 128:], (64, 128))
+        put(AT_QKV + i * 192, qkv[:, i * 128 : (i + 1) * 128])
+    put(AT_REST, qkv[:, 512:], (0, 64))
+    put(AT_REST, proj[:, 128:], (64, 128))
     nst[0:1, :] = norm1[:, :128]
     nst[1:2, 0:64] = norm1[:, 128:]
     nst[2:3, :] = norm2[:, :128]
     nst[3:4, 0:64] = norm2[:, 128:]
-    put(3456, nst[...])
-    copies_b = half_to_core(buf_b, c_b, s_b[0], ny)
-    copies_d = half_to_core(buf_d, c_d, s_d[0], nz)
+    put(AT_NORMS, nst[...])
+    late_y.start()
+    late_z.start()
 
     token_grad = grad_res + grad_in1.astype(BF16).astype(F32)
     exit_token = leave(1, token_grad, s_ext)
 
-    z_a[z] = sum_dealt(piece_of(m2_a, y)[...], copies_a, r3_a)
-    copies_a = share(z_a.at[z], s_a[3], nz, at_z)
-    own_half(buf_b, c_b, m1_b, ny, copies_b)
-    copies_b = deal(lambda i: m1_b.at[i], r2_b, s_b[1], y, ny, at_y)
-    own_half(buf_d, c_d, m1_d, nz, copies_d)
-    copies_d = deal(lambda i: m1_d.at[i], r2_d, s_d[1], z, nz, at_z)
+    early_y.cross()
+    early_z.cross()
+    late_y.deal()
+    late_z.deal()
 
     def fold(h, carry):
         ds = zfold[h]
@@ -398,45 +469,28 @@
     b_s[...] = bst[...].astype(BF16).reshape(nz, rb, 128)
     copies_bias = deal(lambda i: b_s.at[i], b_r1, s_b1, z, nz, at_z)
 
+    z_a[z] = sum_dealt(piece_of(m2_a, y)[...], copies_a, r3_a)
+    copies_a = share(z_a.at[z], s_a[3], nz, at_z)
+    early_y.far()
+    early_z.far()
+    late_y.cross()
+    late_z.cross()
+    b_y[y_hi] = sum_dealt(b_s[z], copies_bias, b_r1)
+    copies_bias = share(b_y.at[y_hi], s_b2, ny_hi, at_yhi)
     mine = core * nx + x
     done = piece_of(fin_a.at[mine], y)
     done[...] = sum_shared(copies_a, z_a, nz)
     copies_a = share(done, s_a[4], ny, at_y)
-    x_b[x] = sum_dealt(m1_b[y], copies_b, r2_b)
-    copies_b = share(x_b.at[x], s_b[2], nx, at_x)
-    x_d[x] = sum_dealt(m1_d[z], copies_d, r2_d)
-    copies_d = share(x_d.at[x], s_d[2], nx, at_x)
-    b_y[y_hi] = sum_dealt(b_s[z], copies_bias, b_r1)
-    copies_bias = share(b_y.at[y_hi], s_b2, ny_hi, at_yhi)
-
+    late_y.far()
+    late_z.far()
+    early_y.gather()
+    early_z.gather()
+    b_fin[z] = sum_shared(copies_bias, b_y, ny_hi)
+    copies_bias = share(b_fin.at[z], s_b3, nz, at_z)
     for copy in copies_a:
         copy.wait()
     copies_a = share(fin_a.at[mine], s_a[5], nx, at_x)
     passed_a = [push(fin_a.at[mine], fin_a.at[mine], s_a[6], 0, at_core())]
-    z_b[z] = sum_shared(copies_b, x_b, nx)
-    copies_b = share(z_b.at[z], s_b[3], nz, at_z)
-    z_d[y] = sum_shared(copies_d, x_d, nx)
-    copies_d = share(z_d.at[y], s_d[3], ny, at_y)
-    b_fin[z] = sum_shared(copies_bias, b_y, ny_hi)
-    copies_bias = share(b_fin.at[z], s_b3, nz, at_z)
-
-    def pass_on(fin, copies, sem, me, count):
-        passed = []
-        for j, copy in enumerate(copies, 1):
-            copy.wait()
-            got = fin.at[core * count + lax.rem(me - j + count, count)]
-            passed.append(push(got, got, sem, j, at_core()))
-        return passed
-
-    def finish(copies, sem, fin, me, slots, count, others, where):
-        own = fin.at[core * count + me]
-        own[...] = sum_shared(copies, slots, others)
-        passed = [push(own, own, sem[5], 0, at_core())]
-        return share(own, sem[4], count, where), passed
-
-    copies_b, passed_b = finish(copies_b, s_b, fin_b, y, z_b, ny, nz, at_y)
-    copies_d, passed_d = finish(copies_d, s_d, fin_d, z, z_d, nz, ny, at_z)
-    passed_a += pass_on(fin_a, copies_a, s_a[6], x, nx)
 
     stores = []
 
@@ -461,6 +515,8 @@
     arrive(1, exit_token, o_token)
 
     store(0, 1)
+    late_y.gather()
+    late_z.gather()
     for copy in copies_bias:
         copy.wait()
     flat = b_fin[...].reshape(256, 128).astype(F32)
@@ -468,8 +524,9 @@
         o_bias[h, :, 0, 0:128] = flat[h * 24 : h * 24 + 23]
         o_bias[h, :, 0, 128:144] = flat[144:167, h * 16 : h * 16 + 16]
     store(5)
-    passed_b += pass_on(fin_b, copies_b, s_b[5], y, ny)
-    passed_d += pass_on(fin_d, copies_d, s_d[5], z, nz)
+    early_y.pass_on()
+    early_z.pass_on()
+    passed_a += pass_on(fin_a, copies_a, s_a[6], x, nx)
 
     scale = float(cells) ** (-0.5)
 
@@ -481,25 +538,27 @@
         whole = parts[0] if len(parts) == 1 else jnp.concatenate(parts, axis=0)
         return whole.astype(F32) * scale
 
+    early_y.wait()
+    early_z.wait()
     for copy in passed_a:
         copy.wait()
     for i in range(6):
-        o_up[:, pl.ds(i * 128, 128)] = take(i * 192, 192)
+        o_up[:, pl.ds(i * 128, 128)] = take(AT_UP + i * 192, 192)
     store(7)
-    for copy in passed_b:
-        copy.wait()
     for i in range(6):
-        o_down[:, pl.ds(i * 128, 128)] = take(1152 + i * 192, 192)
+        o_down[:, pl.ds(i * 128, 128)] = take(AT_DOWN + i * 192, 192)
     store(8)
-    for copy in passed_d:
-        copy.wait()
+    o_proj[:, 0:128] = take(AT_PROJ, 192)
+    late_y.pass_on()
+    late_z.pass_on()
+    late_y.wait()
+    late_z.wait()
     for i in range(4):
-        o_qkv[:, pl.ds(i * 128, 128)] = take(2304 + i * 192, 192)
-    o_proj[:, 0:128] = take(3072, 192)
-    rest = take(3264, 192)
+        o_qkv[:, pl.ds(i * 128, 128)] = take(AT_QKV + i * 192, 192)
+    rest = take(AT_REST, 192)
     o_qkv[:, 512:576] = rest[:, :64]
     o_proj[:, 128:192] = rest[:, 64:]
-    rest = take(3456, 16)
+    rest = take(AT_NORMS, 16)
     o_n1[:, 0:128] = rest[0:1, :]
     o_n1[:, 128:192] = rest[1:2, :64]
     o_n2[:, 0:128] = rest[2:3, :]
@@ -511,7 +570,8 @@
 
 def piece_rows(geo):
     nlat, nlon, ny_lo, nx, nz, ny_hi = geo
-    return ROWS[0] // (2 * nx), ROWS[1] // (2 * ny_lo * ny_hi), ROWS[2] // (2 * nz)
+    counts = (nx, ny_lo * ny_hi, nz, ny_lo * ny_hi, nz)
+    return tuple(rows // (2 * count) for rows, count in zip(ROWS, counts))
 
 
 def spread(*refs):
@@ -532,7 +592,7 @@
 def on_device(geo, tokens, labels, gain1, wqkv, wproj, table, gain2, wup, wdown, cotangent):
     nlat, nlon, ny_lo, nx, nz, ny_hi = geo
     ny = ny_lo * ny_hi
-    pa, pb, pd = piece_rows(geo)
+    pa, *flat_rows = piece_rows(geo)
     rb = 256 // nz
     vmem = pltpu.VMEM
     args = (
@@ -553,9 +613,9 @@
     )
     scratch = [vmem(arg.shape, arg.dtype) for arg in args + shapes]
     scratch += [
-        vmem((4, 16, HALF), F32),
-        vmem((3, 16, HALF), BF16),
-        vmem((3, 16, HALF), BF16),
+        vmem((2, 4, 16, HOLD), F32),
+        vmem((2, 3, 16, HOLD), BF16),
+        vmem((2, 3, 16, HOLD), BF16),
         vmem((192, C), F32),
         vmem((192, C), F32),
         vmem((16, 128), F32),
@@ -583,7 +643,7 @@
         vmem((nz, pa // ny, 128), BF16),
         vmem((2 * nx, pa, 128), BF16),
     ]
-    for first, piece, last in ((ny, pb, nz), (nz, pd, ny)):
+    for piece, first, last in zip(flat_rows, (ny, nz, ny, nz), (nz, ny, nz, ny)):
         scratch += [
             vmem((2 * first, piece, 128), BF16),
             vmem((first, piece, 128), BF16),
@@ -597,10 +657,10 @@
         pltpu.SemaphoreType.DMA((10,)),
         pltpu.SemaphoreType.DMA((9,)),
     ]
-    counts = [3, 3, 3, nz - 1, ny_hi - 1, nz - 1]
+    counts = [3, 3, 3, 3, nz - 1, ny_hi - 1, nz - 1]
     counts += [1, nx - 1, ny - 1, nz - 1, ny - 1, nx - 1, nx]
-    counts += [1, ny - 1, nx - 1, nz - 1, ny - 1, ny]
-    counts += [1, nz - 1, nx - 1, ny - 1, nz - 1, nz]
+    for first, last in ((ny, nz), (nz, ny)) * 2:
+        counts += [1, first - 1, nx - 1, last - 1, first - 1, first]
     for count in counts:
         scratch += [pltpu.SemaphoreType.DMA((count,)), pltpu.SemaphoreType.DMA((count,))]
     anywhere = pl.BlockSpec(memory_space=pl.ANY)

time: 66.7 us -> 62.1 us (0.931)
  Pallas kernels: 65.9 us -> 61.2 us
    pallas_call x1, Pallas kernels: 63.4 us -> 58.7 us  [on_device(): pl.pallas_call(functools.partial(kernel, geo), out_shape=shapes, in_specs...]
where the time goes in v3:
time: 62.1 us; the launch traced here: 61.9 us
  Pallas kernels  61.2 us (99%)
  between operations  0.65 us (1%)
    pallas_call x1, Pallas kernels, on_device(): pl.pallas_call(functools.partial(kernel, geo), out_shape=shapes, in_specs...  58.7 us
    pallas_call x1, Pallas kernels, on_device(): pl.pallas_call(spread, out_shape=shapes, in_specs=[anywhere] * 9, out_spe...  2.54 us

profile of v3, /device:TPU:1, one launch (start us, length us, event | category | flops | bytes accessed | tf_op | source)
XLA Modules:
  0.0 61.9 jit_solution(14292039100384460031)
XLA Ops:
  0.6 58.7 %shard_map.169 = (bf16[6,2,2304]{2,1,0:T(2,128)(2,1)}, bf16[6,2,2304]{2,1,0:T(2,128)(2,1)}, f32[1,192]{1,0:T(1,128)}, f32[192,576]{1,0:T(8,128)}, f32[192,192]{1...) custom-call(bf16[6,2,2304]{2,1,0:T(2,128)(2,1)} %bitcast.15, ...), custom_call_target="tpu_custom_call" | custom-call | tf_op jit(solution)/shard_map/pallas_call | solution.py:667
  59.4 2.5 %shard_map.170 = (bf16[6,2,2304]{2,1,0:T(2,128)(2,1)}, bf16[6,2,2304]{2,1,0:T(2,128)(2,1)}, f32[1,192]{1,0:T(1,128)}, f32[192,576]{1,0:T(8,128)}, f32[192,192]{1...) custom-call(bf16[6,2,2304]{2,1,0:T(2,128)(2,1)} %get-tuple-element.27.refs_, ...), custom_call_target="tpu_custom_call" | custom-call | tf_op jit(solution)/shard_map/pallas_call | solution.py:677

commit v4 on v3

--- a/solution.py
+++ b/solution.py
@@ -171,10 +171,6 @@
         ]
 
     entry = enter(0, s_ent)
-    loads[9].wait()
-    quarters(1, cot)
-    entry2 = enter(1, s_ent2)
-
     loads[1].wait()
     loads[5].wait()
 
@@ -221,7 +217,11 @@
         bias[h] = jnp.where(same, out, MASKED)
         return carry
 
-    lax.fori_loop(0, HEADS, build, 0)
+    lax.fori_loop(0, HEADS // 2, build, 0)
+    loads[9].wait()
+    quarters(1, cot)
+    entry2 = enter(1, s_ent2)
+    lax.fori_loop(HEADS // 2, HEADS, build, 0)
     for i in (2, 4):
         bufs[i][...] = jnp.zeros_like(bufs[i])
     nst[...] = jnp.zeros_like(nst)
@@ -310,19 +310,23 @@
         for i in range(count):
             out[i] = (buf[core * count + i].astype(F32) + other[i].astype(F32)).astype(BF16)
 
+    def far_first(count):
+        return sorted(range(1, count), key=lambda j: -min(j, count - j))
+
     def deal(pieces, slots, sem, me, count, where):
         return [
             push(pieces(lax.rem(me + j, count)), slots.at[j - 1], sem, j - 1, where(j))
-            for j in range(1, count)
+            for j in far_first(count)
         ]
 
     def share(ref, sem, count, where):
-        return [push(ref, ref, sem, j - 1, where(j)) for j in range(1, count)]
+        return [push(ref, ref, sem, j - 1, where(j)) for j in far_first(count)]
 
     def sum_dealt(own, copies, slots):
         total = own.astype(F32)
-        for i, copy in enumerate(copies):
+        for copy in copies:
             copy.wait()
+        for i in range(len(copies)):
             total = total + slots[i].astype(F32)
         return total.astype(BF16)
 
@@ -336,7 +340,7 @@
 
     def pass_on(fin, copies, sem, me, count):
         passed = []
-        for j, copy in enumerate(copies, 1):
+        for j, copy in reversed(list(zip(far_first(count), copies))):
             copy.wait()
             got = fin.at[core * count + lax.rem(me - j + count, count)]
             passed.append(push(got, got, sem, j, at_core()))
@@ -417,15 +421,12 @@
         dv = dv + tn(p.astype(BF16), gm)
         dk = dk + tn(ds, q * masks[h])
         dq = dq + nn(ds, k * masks[h])
-        if h == 0:
+        if h == 2:
             own_half(buf_a, c_a, m1_a, nx, copies_a)
             copies_a = deal(lambda i: m1_a.at[i], r2_a, s_a[1], x, nx, at_x)
             early_y.deal()
-        if h == 1:
+        if h == 5:
             early_z.deal()
-        if h == 5:
-            m2_a[...] = sum_dealt(m1_a[x], copies_a, r2_a)
-            copies_a = deal(lambda i: piece_of(m2_a, i), r3_a, s_a[2], y, ny, at_y)
     grad_packed = jnp.concatenate([dq, dk, dv], axis=1).astype(BF16)
     qkv = tn(n1, grad_packed)
     grad_n1 = nt(grad_packed, wqkv[...])
@@ -446,11 +447,6 @@
     token_grad = grad_res + grad_in1.astype(BF16).astype(F32)
     exit_token = leave(1, token_grad, s_ext)
 
-    early_y.cross()
-    early_z.cross()
-    late_y.deal()
-    late_z.deal()
-
     def fold(h, carry):
         ds = zfold[h]
         ffold[...] = jnp.zeros_like(ffold)
@@ -461,7 +457,14 @@
         fsum[h, 0:23, :] = jnp.sum(wide, axis=1) * (1.0 / SCALE)
         return carry
 
-    lax.fori_loop(0, HEADS, fold, 0)
+    lax.fori_loop(0, HEADS // 2, fold, 0)
+    late_y.deal()
+    late_z.deal()
+    m2_a[...] = sum_dealt(m1_a[x], copies_a, r2_a)
+    copies_a = deal(lambda i: piece_of(m2_a, i), r3_a, s_a[2], y, ny, at_y)
+    early_y.cross()
+    early_z.cross()
+    lax.fori_loop(HEADS // 2, HEADS, fold, 0)
     for h in range(HEADS):
         bst[pl.ds(h * 24, 23), :] = fsum[h, 0:23, 0:128]
         bst[pl.ds(144, 23), pl.ds(h * 16, 16)] = fsum[h, 0:23, 128:144]
@@ -471,10 +474,10 @@
 
     z_a[z] = sum_dealt(piece_of(m2_a, y)[...], copies_a, r3_a)
     copies_a = share(z_a.at[z], s_a[3], nz, at_z)
+    late_y.cross()
+    late_z.cross()
     early_y.far()
     early_z.far()
-    late_y.cross()
-    late_z.cross()
     b_y[y_hi] = sum_dealt(b_s[z], copies_bias, b_r1)
     copies_bias = share(b_y.at[y_hi], s_b2, ny_hi, at_yhi)
     mine = core * nx + x
@@ -487,11 +490,6 @@
     early_z.gather()
     b_fin[z] = sum_shared(copies_bias, b_y, ny_hi)
     copies_bias = share(b_fin.at[z], s_b3, nz, at_z)
-    for copy in copies_a:
-        copy.wait()
-    copies_a = share(fin_a.at[mine], s_a[5], nx, at_x)
-    passed_a = [push(fin_a.at[mine], fin_a.at[mine], s_a[6], 0, at_core())]
-
     stores = []
 
     def store(*which):
@@ -517,6 +515,10 @@
     store(0, 1)
     late_y.gather()
     late_z.gather()
+    for copy in copies_a:
+        copy.wait()
+    copies_a = share(fin_a.at[mine], s_a[5], nx, at_x)
+    passed_a = [push(fin_a.at[mine], fin_a.at[mine], s_a[6], 0, at_core())]
     for copy in copies_bias:
         copy.wait()
     flat = b_fin[...].reshape(256, 128).astype(F32)
@@ -527,6 +529,8 @@
     early_y.pass_on()
     early_z.pass_on()
     passed_a += pass_on(fin_a, copies_a, s_a[6], x, nx)
+    late_y.pass_on()
+    late_z.pass_on()
 
     scale = float(cells) ** (-0.5)
 
@@ -549,8 +553,6 @@
         o_down[:, pl.ds(i * 128, 128)] = take(AT_DOWN + i * 192, 192)
     store(8)
     o_proj[:, 0:128] = take(AT_PROJ, 192)
-    late_y.pass_on()
-    late_z.pass_on()
     late_y.wait()
     late_z.wait()
     for i in range(4):

time: 62.1 us -> 60 us (0.966)
  Pallas kernels: 61.2 us -> 59.2 us
    pallas_call x1, Pallas kernels: 58.7 us -> 56.7 us  [on_device(): pl.pallas_call(functools.partial(kernel, geo), out_shape=shapes, in_specs...]
where the time goes in v4:
time: 60 us; the launch traced here: 59.8 us
  Pallas kernels  59.2 us (99%)
  between operations  0.65 us (1%)
    pallas_call x1, Pallas kernels, on_device(): pl.pallas_call(functools.partial(kernel, geo), out_shape=shapes, in_specs...  56.7 us
    pallas_call x1, Pallas kernels, on_device(): pl.pallas_call(spread, out_shape=shapes, in_specs=[anywhere] * 9, out_spe...  2.54 us

profile of v4, /device:TPU:1, one launch (start us, length us, event | category | flops | bytes accessed | tf_op | source)
XLA Modules:
  0.0 59.8 jit_solution(605604195160681422)
XLA Ops:
  0.6 56.7 %shard_map.169 = (bf16[6,2,2304]{2,1,0:T(2,128)(2,1)}, bf16[6,2,2304]{2,1,0:T(2,128)(2,1)}, f32[1,192]{1,0:T(1,128)}, f32[192,576]{1,0:T(8,128)}, f32[192,192]{1...) custom-call(bf16[6,2,2304]{2,1,0:T(2,128)(2,1)} %bitcast.15, ...), custom_call_target="tpu_custom_call" | custom-call | tf_op jit(solution)/shard_map/pallas_call | solution.py:669
  57.3 2.5 %shard_map.170 = (bf16[6,2,2304]{2,1,0:T(2,128)(2,1)}, bf16[6,2,2304]{2,1,0:T(2,128)(2,1)}, f32[1,192]{1,0:T(1,128)}, f32[192,576]{1,0:T(8,128)}, f32[192,192]{1...) custom-call(bf16[6,2,2304]{2,1,0:T(2,128)(2,1)} %get-tuple-element.27.refs_, ...), custom_call_target="tpu_custom_call" | custom-call | tf_op jit(solution)/shard_map/pallas_call | solution.py:679

commit v5 on v4

--- a/solution.py
+++ b/solution.py
@@ -80,15 +80,11 @@
     tok, lab, g1, wqkv, wproj, btab, g2, wup, wdown, cot = held
     o_block, o_token, o_n1, o_qkv, o_proj, o_bias, o_n2, o_up, o_down = ready
     (
-        stage, ent_s, ent_r, xs, gs, labs, ytab, bias, probs, ex_s, ex_r, rows_st,
+        stage, ent_s, ent_r, xs, gs, labs, ytab, bias, probs, ex_st, ex_s, ex_r, rows_st,
         nst, zfold, ffold, fsum, bst, b_s, b_r1, b_y, b_fin,
         buf_a, c_a, m1_a, r2_a, m2_a, r3_a, z_a, fin_a, *flat_refs,
-    ) = refs[:57]
-    in_sem, out_sem, *sems = refs[57:]
-    loads = {}
-    for i in (0, 9, 1, 5, 2, 3, 4, 6, 7, 8):
-        loads[i] = pltpu.make_async_copy(inputs[i], held[i], in_sem.at[i])
-        loads[i].start()
+    ) = refs[:58]
+    in_sem, out_sem, *sems = refs[58:]
     nlat, nlon, ny_lo, nx, nz, ny_hi = geo
     ny = ny_lo * ny_hi
     per = piece_rows(geo)
@@ -137,17 +133,22 @@
         return copy
 
     barrier = pltpu.get_barrier_semaphore()
-    partners = [at_core()]
+    partners = [near(-1, 0), near(0, -1), near(-1, -1), near(1, 0), near(0, 1), near(1, 1)]
+    partners += [at_core()]
     partners += [at_x(k) for k in range(1, nx)]
     partners += [at_y(k) for k in range(1, ny)]
     partners += [at_z(k) for k in range(1, nz)]
-    partners += [near(-1, 0), near(0, -1), near(-1, -1), near(1, 0), near(0, 1), near(1, 1)]
     for dev in partners:
         pl.semaphore_signal(barrier, inc=1, device_id=dev, device_id_type=MESH)
+    loads = {}
+    for i in (0, 9, 1, 5, 2, 3, 4, 6, 7, 8):
+        loads[i] = pltpu.make_async_copy(inputs[i], held[i], in_sem.at[i])
+        loads[i].start()
 
     loads[0].wait()
 
     stage[...] = jnp.zeros_like(stage)
+    ex_st[...] = jnp.zeros_like(ex_st)
 
     def quarters(kind, ref):
         for half in range(2):
@@ -276,10 +277,12 @@
         for half in range(2):
             for part in range(2):
                 i = half * 2 + part
-                out = ex_r.at[which, 0] if i == 0 else ex_s.at[which, i]
                 for c in range(6):
                     row = (11 - part * 6 - c) * 16 + half * 8
-                    out[:, pl.ds(c * C, C)] = rows_st[pl.ds(row, 8), :]
+                    side, column = c // 3, c % 3
+                    ex_st[i, pl.ds(side * 8, 8), pl.ds(column * C, C)] = rows_st[pl.ds(row, 8), :]
+                out = ex_s if i else ex_r
+                out[which, i] = ex_st[i].astype(BF16)
                 if i:
                     copies.append(
                         push(ex_s.at[which, i], ex_r.at[which, i], sem, i - 1, near(half, part))
@@ -504,10 +507,13 @@
         for half in range(2):
             for part in range(2):
                 i = (1 - half) * 2 + 1 - part
+                rows = ex_r[which, i].astype(F32)
                 for row in range(3):
-                    out[half * 3 + row, :, pl.ds(part * HALF, HALF)] = ex_r[
-                        which, i, pl.ds(row * 2, 2), :
-                    ].astype(BF16)
+                    for side in range(2):
+                        place = pl.ds(part * HALF + side * 576, 576)
+                        out[half * 3 + row, :, place] = rows[
+                            side * 8 + row * 2 : side * 8 + row * 2 + 2, 0:576
+                        ].astype(BF16)
 
     arrive(0, exit_block, o_block)
     arrive(1, exit_token, o_token)
@@ -624,8 +630,9 @@
         vmem((368, 192), F32),
         vmem((HEADS, 192, 192), F32),
         vmem((HEADS, 192, 192), F32),
-        vmem((2, 4, 8, HALF), F32),
-        vmem((2, 4, 8, HALF), F32),
+        vmem((4, 16, HOLD), F32),
+        vmem((2, 4, 16, HOLD), BF16),
+        vmem((2, 4, 16, HOLD), BF16),
         vmem((192, C), F32),
         vmem((16, 128), F32),
         vmem((HEADS, 192, 192), BF16),

time: 60 us -> 58.6 us (0.977)
  Pallas kernels: 59.2 us -> 57.8 us
    pallas_call x1, Pallas kernels: 56.7 us -> 55.3 us  [on_device(): pl.pallas_call(functools.partial(kernel, geo), out_shape=shapes, in_specs...]
where the time goes in v5:
time: 58.6 us; the launch traced here: 58.5 us
  Pallas kernels  57.8 us (99%)
  between operations  0.65 us (1%)
    pallas_call x1, Pallas kernels, on_device(): pl.pallas_call(functools.partial(kernel, geo), out_shape=shapes, in_specs...  55.3 us
    pallas_call x1, Pallas kernels, on_device(): pl.pallas_call(spread, out_shape=shapes, in_specs=[anywhere] * 9, out_spe...  2.54 us

profile of v5, /device:TPU:1, one launch (start us, length us, event | category | flops | bytes accessed | tf_op | source)
XLA Modules:
  0.0 58.5 jit_solution(9102160389371854159)
XLA Ops:
  0.6 55.3 %shard_map.169 = (bf16[6,2,2304]{2,1,0:T(2,128)(2,1)}, bf16[6,2,2304]{2,1,0:T(2,128)(2,1)}, f32[1,192]{1,0:T(1,128)}, f32[192,576]{1,0:T(8,128)}, f32[192,192]{1...) custom-call(bf16[6,2,2304]{2,1,0:T(2,128)(2,1)} %bitcast.15, ...), custom_call_target="tpu_custom_call" | custom-call | tf_op jit(solution)/shard_map/pallas_call | solution.py:676
  55.9 2.5 %shard_map.170 = (bf16[6,2,2304]{2,1,0:T(2,128)(2,1)}, bf16[6,2,2304]{2,1,0:T(2,128)(2,1)}, f32[1,192]{1,0:T(1,128)}, f32[192,576]{1,0:T(8,128)}, f32[192,192]{1...) custom-call(bf16[6,2,2304]{2,1,0:T(2,128)(2,1)} %get-tuple-element.27.refs_, ...), custom_call_target="tpu_custom_call" | custom-call | tf_op jit(solution)/shard_map/pallas_call | solution.py:686

commit v6 on v5

--- a/solution.py
+++ b/solution.py
@@ -460,14 +460,14 @@
         fsum[h, 0:23, :] = jnp.sum(wide, axis=1) * (1.0 / SCALE)
         return carry
 
-    lax.fori_loop(0, HEADS // 2, fold, 0)
+    lax.fori_loop(0, 1, fold, 0)
     late_y.deal()
     late_z.deal()
     m2_a[...] = sum_dealt(m1_a[x], copies_a, r2_a)
     copies_a = deal(lambda i: piece_of(m2_a, i), r3_a, s_a[2], y, ny, at_y)
     early_y.cross()
     early_z.cross()
-    lax.fori_loop(HEADS // 2, HEADS, fold, 0)
+    lax.fori_loop(1, HEADS, fold, 0)
     for h in range(HEADS):
         bst[pl.ds(h * 24, 23), :] = fsum[h, 0:23, 0:128]
         bst[pl.ds(144, 23), pl.ds(h * 16, 16)] = fsum[h, 0:23, 128:144]

time: 58.6 us -> 59.2 us (1.010)
  Pallas kernels: 57.8 us -> 58.4 us
where the time goes in v6:
time: 59.2 us; the launch traced here: 59 us
  Pallas kernels  58.4 us (99%)
  between operations  0.65 us (1%)
    pallas_call x1, Pallas kernels, on_device(): pl.pallas_call(functools.partial(kernel, geo), out_shape=shapes, in_specs...  55.8 us
    pallas_call x1, Pallas kernels, on_device(): pl.pallas_call(spread, out_shape=shapes, in_specs=[anywhere] * 9, out_spe...  2.54 us

profile of v6, /device:TPU:1, one launch (start us, length us, event | category | flops | bytes accessed | tf_op | source)
XLA Modules:
  0.0 59.0 jit_solution(12198159786847233135)
XLA Ops:
  0.6 55.8 %shard_map.169 = (bf16[6,2,2304]{2,1,0:T(2,128)(2,1)}, bf16[6,2,2304]{2,1,0:T(2,128)(2,1)}, f32[1,192]{1,0:T(1,128)}, f32[192,576]{1,0:T(8,128)}, f32[192,192]{1...) custom-call(bf16[6,2,2304]{2,1,0:T(2,128)(2,1)} %bitcast.15, ...), custom_call_target="tpu_custom_call" | custom-call | tf_op jit(solution)/shard_map/pallas_call | solution.py:676
  56.5 2.5 %shard_map.170 = (bf16[6,2,2304]{2,1,0:T(2,128)(2,1)}, bf16[6,2,2304]{2,1,0:T(2,128)(2,1)}, f32[1,192]{1,0:T(1,128)}, f32[192,576]{1,0:T(8,128)}, f32[192,192]{1...) custom-call(bf16[6,2,2304]{2,1,0:T(2,128)(2,1)} %get-tuple-element.27.refs_, ...), custom_call_target="tpu_custom_call" | custom-call | tf_op jit(solution)/shard_map/pallas_call | solution.py:686
